TPU v7x, 32 devices: a whole 2x2x4 slice. The times are simulated.
32 devices in a mesh: dp: 4 (over x, core), ctx: 8 (over z, y).
Axes of the slice: x: 2, y: 2, z: 4, core: 2. Of those that a mesh axis runs over, the one named last changes fastest.
Arguments:
- hidden_in: bfloat16 [4, 4, 512, 1024], P(None, 'dp', 'ctx'), may hold values from -6 to 6
- segments: int32 [4, 4, 512], P(None, 'dp', 'ctx'), may hold values from 0 to 5, as said below
- attention_gain: bfloat16 [1024], P(('dp', 'ctx')), may hold values from 0.099609375 to 1.8984375
- query_gain: bfloat16 [128], P(('dp', 'ctx')), may hold values from 0.59765625 to 2
- key_gain: bfloat16 [128], P(('dp', 'ctx')), may hold values from 0.59765625 to 2
- query_weight: bfloat16 [1024, 2048], P(('dp', 'ctx')), may hold values from -0.1875 to 0.1875
- key_weight: bfloat16 [1024, 1024], P(('dp', 'ctx')), may hold values from -0.1875 to 0.1875
- value_weight: bfloat16 [1024, 1024], P(('dp', 'ctx')), may hold values from -0.1875 to 0.1875
- out_weight: bfloat16 [2048, 1024], P(None, ('dp', 'ctx')), may hold values from -0.75 to 0.75
- feedforward_gain: bfloat16 [1024], P(('dp', 'ctx')), may hold values from 0.099609375 to 1.8984375
- gate_weight: bfloat16 [1024, 3072], P(('dp', 'ctx')), may hold values from -0.1875 to 0.1875
- up_weight: bfloat16 [1024, 3072], P(('dp', 'ctx')), may hold values from -0.1875 to 0.1875
- down_weight: bfloat16 [3072, 1024], P(None, ('dp', 'ctx')), may hold values from -0.109375 to 0.109375
- cotangent: bfloat16 [4, 4, 512, 1024], P(None, 'dp', 'ctx'), may hold values from -6 to 6
Outputs:
- block_out: bfloat16 [4, 4, 512, 1024], P(None, 'dp', 'ctx')
- input_grad: float32 [4, 4, 512, 1024], P(None, 'dp', 'ctx')
- attention_gain_grad: float32 [1024], P(('dp', 'ctx'))
- query_gain_grad: float32 [128], P(('dp', 'ctx'))
- key_gain_grad: float32 [128], P(('dp', 'ctx'))
- query_weight_grad: float32 [1024, 2048], P(('dp', 'ctx'))
- key_weight_grad: float32 [1024, 1024], P(('dp', 'ctx'))
- value_weight_grad: float32 [1024, 1024], P(('dp', 'ctx'))
- out_weight_grad: float32 [2048, 1024], P(None, ('dp', 'ctx'))
- feedforward_gain_grad: float32 [1024], P(('dp', 'ctx'))
- gate_weight_grad: float32 [1024, 3072], P(('dp', 'ctx'))
- up_weight_grad: float32 [1024, 3072], P(('dp', 'ctx'))
- down_weight_grad: float32 [3072, 1024], P(None, ('dp', 'ctx'))
Inputs may be any that keep to these rules, and one draw needn't show every extreme that they name: `segments`: along every sequence the segment number starts at 0 and rises by 0 or 1 from one token to the next. Of the 4 sequences that share an index of dp, one is a single document; each of the others holds exactly six documents.
All inputs are finite; a program needn't handle non-finite values.
Results may differ from a plain program's by a relative error of at most 0.019.
Values may be sent and summed in bfloat16 or wider, within the bound.
A program may use at most 256 MiB of HBM per device.

v0:
```python
import jax
import jax.numpy as jnp
from jax import lax
from jax.sharding import PartitionSpec as P

D = 1024
HQ = 16
HK = 8
HD = 128
FF = 3072
MB = 4


NORM_EPS = 1e-06
ROPE_BASE = 1000000.0
MASKED = -1e30


def normalize(value):
    return value * lax.rsqrt(jnp.mean(value * value, axis=-1, keepdims=True) + NORM_EPS)


def norm_back(value, grad):
    scale = lax.rsqrt(jnp.mean(value * value, axis=-1, keepdims=True) + NORM_EPS)
    return scale * grad - value * (scale * scale * scale) * jnp.mean(
        grad * value, axis=-1, keepdims=True
    )


def rope_tables(first, count):
    positions = (first + jnp.arange(count, dtype=jnp.int32)).astype(jnp.float32)
    frequency = ROPE_BASE ** (-(jnp.arange(HD // 2, dtype=jnp.float32) * 2.0) / HD)
    angles = positions[:, None] * frequency[None, :]
    cosine = jnp.concatenate([jnp.cos(angles), jnp.cos(angles)], axis=-1)
    sine = jnp.concatenate([jnp.sin(angles), jnp.sin(angles)], axis=-1)
    return (cosine[:, None, :], sine[:, None, :])


def rotate(value, cosine, sine):
    half = value.shape[-1] // 2
    turned = jnp.concatenate([-value[..., half:], value[..., :half]], axis=-1)
    return value * cosine + turned * sine


def rotate_back(grad, cosine, sine):
    half = grad.shape[-1] // 2
    scaled = grad * sine
    return grad * cosine + jnp.concatenate([scaled[..., half:], -scaled[..., :half]], axis=-1)


def contract_last(left, right):
    return lax.dot_general(
        left, right, (((1,), (1,)), ((), ())), preferred_element_type=jnp.float32
    )


def contract_first(left, right):
    return lax.dot_general(
        left, right, (((0,), (0,)), ((), ())), preferred_element_type=jnp.float32
    )


def block_rows(rows):
    size = min(rows, 512)
    while rows % size:
        size -= 1
    return size


def fetch_attention(
    attention_gain, query_gain, key_gain, query_weight, key_weight, value_weight, out_weight
):
    return (
        lax.all_gather(attention_gain, ("dp", "ctx"), axis=0, tiled=True),
        lax.all_gather(query_gain, ("dp", "ctx"), axis=0, tiled=True),
        lax.all_gather(key_gain, ("dp", "ctx"), axis=0, tiled=True),
        lax.all_gather(query_weight, ("dp", "ctx"), axis=0, tiled=True),
        lax.all_gather(key_weight, ("dp", "ctx"), axis=0, tiled=True),
        lax.all_gather(value_weight, ("dp", "ctx"), axis=0, tiled=True),
        lax.all_gather(out_weight, ("dp", "ctx"), axis=1, tiled=True),
    )


def fetch_feedforward(feedforward_gain, gate_weight, up_weight, down_weight):
    return (
        lax.all_gather(feedforward_gain, ("dp", "ctx"), axis=0, tiled=True),
        lax.all_gather(gate_weight, ("dp", "ctx"), axis=0, tiled=True),
        lax.all_gather(up_weight, ("dp", "ctx"), axis=0, tiled=True),
        lax.all_gather(down_weight, ("dp", "ctx"), axis=1, tiled=True),
    )


def over_blocks(state, pieces, update):
    rows = pieces[0].shape[0]
    size = block_rows(rows)
    count = rows // size
    stacked = tuple((piece.reshape((count, size) + piece.shape[1:]) for piece in pieces))
    offsets = size * jnp.arange(count, dtype=jnp.int32)

    def step(current, item):
        block = item[:-1]
        offset = item[-1]
        current = update(current, block, offset)
        return (current, None)

    final, unused = lax.scan(step, state, stacked + (offsets,))
    return final


def on_device(
    hidden_in,
    segments,
    attention_gain,
    query_gain,
    key_gain,
    query_weight,
    key_weight,
    value_weight,
    out_weight,
    feedforward_gain,
    gate_weight,
    up_weight,
    down_weight,
    cotangent,
):
    tokens = hidden_in.shape[2]
    groups = HQ // HK
    scale = HD ** (-0.5)
    first = lax.axis_index("ctx") * tokens
    length = lax.axis_size("ctx") * tokens
    query_pos = first + jnp.arange(tokens, dtype=jnp.int32)
    cosine, sine = rope_tables(first, tokens)
    attention_shards = (
        attention_gain,
        query_gain,
        key_gain,
        query_weight,
        key_weight,
        value_weight,
        out_weight,
    )
    feed_shards = (feedforward_gain, gate_weight, up_weight, down_weight)
    grad_attention_gain = jnp.zeros((D,), jnp.float32)
    grad_feed_gain = jnp.zeros((D,), jnp.float32)
    grad_query_gain = jnp.zeros((HD,), jnp.float32)
    grad_key_gain = jnp.zeros((HD,), jnp.float32)
    outputs = []
    input_grads = []
    stored = []
    for batch in range(MB):
        hidden = hidden_in[batch, 0].astype(jnp.float32)
        query_seg = segments[batch, 0]
        grad_out = cotangent[batch, 0]
        attention_set = fetch_attention(*attention_shards)
        gain_in, gain_query, gain_key, whole_query, whole_key, whole_value, whole_out = (
            attention_set
        )
        normed = normalize(hidden)
        scaled_in = (normed * gain_in.astype(jnp.float32)).astype(jnp.bfloat16)
        query_heads = jnp.dot(scaled_in, whole_query, preferred_element_type=jnp.float32).reshape(
            tokens, HQ, HD
        )
        key_heads = jnp.dot(scaled_in, whole_key, preferred_element_type=jnp.float32).reshape(
            tokens, HK, HD
        )
        values = jnp.dot(scaled_in, whole_value, preferred_element_type=jnp.float32).astype(
            jnp.bfloat16
        )
        query_norm = normalize(query_heads)
        key_norm = normalize(key_heads)
        query_scale = gain_query.astype(jnp.float32)
        key_scale = gain_key.astype(jnp.float32)
        queries = rotate(query_norm * query_scale, cosine, sine).astype(jnp.bfloat16)
        keys_low = rotate(key_norm * key_scale, cosine, sine).astype(jnp.bfloat16)
        grouped = queries.reshape(tokens, HK, groups, HD)
        keys_flat = keys_low.reshape(tokens, HK * HD)

        def key_scores(keys, key_seg, offset):
            rows = keys.shape[0]
            shaped = keys.reshape(rows, HK, HD)
            raw = (
                jnp.einsum("qkgd,skd->kgqs", grouped, shaped, preferred_element_type=jnp.float32)
                * scale
            )
            key_pos = offset + jnp.arange(rows, dtype=jnp.int32)
            visible = (key_pos[None, :] <= query_pos[:, None]) & (
                key_seg[None, :] == query_seg[:, None]
            )
            return (jnp.where(visible, raw, MASKED), visible, shaped)

        def fold_with(update, state, pieces):
            return over_blocks(state, pieces, update)

        def add_lse(state, block, offset):
            keys, key_seg = block
            masked, visible, shaped = key_scores(keys, key_seg, offset)
            top, total = state
            new_top = jnp.maximum(top, jnp.max(masked, axis=-1))
            terms = jnp.where(visible, jnp.exp(masked - new_top[..., None]), 0.0)
            return (new_top, total * jnp.exp(top - new_top) + jnp.sum(terms, axis=-1))

        start_state = (
            jnp.full((HK, groups, tokens), MASKED, jnp.float32),
            jnp.zeros((HK, groups, tokens), jnp.float32),
        )
        top, total = fold_with(
            add_lse,
            start_state,
            (
                lax.all_gather(keys_flat, "ctx", axis=0, tiled=True),
                lax.all_gather(query_seg, "ctx", axis=0, tiled=True),
            ),
        )
        lse = top + jnp.log(total)

        def add_mixed(state, block, offset):
            keys, values_block, key_seg = block
            masked, visible, shaped = key_scores(keys, key_seg, offset)
            probs = jnp.exp(masked - lse[..., None]).astype(jnp.bfloat16)
            value_heads = values_block.reshape(values_block.shape[0], HK, HD)
            return state + jnp.einsum(
                "kgqs,skd->qkgd", probs, value_heads, preferred_element_type=jnp.float32
            )

        mixed = fold_with(
            add_mixed,
            jnp.zeros((tokens, HK, groups, HD), jnp.float32),
            (
                lax.all_gather(keys_flat, "ctx", axis=0, tiled=True),
                lax.all_gather(values, "ctx", axis=0, tiled=True),
                lax.all_gather(query_seg, "ctx", axis=0, tiled=True),
            ),
        )
        mixed_low = mixed.reshape(tokens, HQ * HD).astype(jnp.bfloat16)
        residual = hidden + jnp.dot(mixed_low, whole_out, preferred_element_type=jnp.float32)
        feed_set = fetch_feedforward(*feed_shards)
        gain_feed, whole_gate, whole_up, whole_down = feed_set
        feed_normed = normalize(residual)
        feed_scale = gain_feed.astype(jnp.float32)
        ff_in = (feed_normed * feed_scale).astype(jnp.bfloat16)
        gate = jnp.dot(ff_in, whole_gate, preferred_element_type=jnp.float32)
        up_part = jnp.dot(ff_in, whole_up, preferred_element_type=jnp.float32)
        sigmoid = jax.nn.sigmoid(gate)
        swish = gate * sigmoid
        hidden_low = (swish * up_part).astype(jnp.bfloat16)
        block_out = residual + jnp.dot(hidden_low, whole_down, preferred_element_type=jnp.float32)
        outputs.append(block_out.astype(jnp.bfloat16))
        feed_back = fetch_feedforward(*feed_shards)
        attention_back = fetch_attention(*attention_shards)
        back_gain_feed, back_gate, back_up, back_down = feed_back
        back_gain_in, back_gain_query, back_gain_key, back_query, back_key, back_value, back_out = (
            attention_back
        )
        grad_hidden = contract_last(grad_out, back_down)
        grad_gate = (grad_hidden * up_part * (sigmoid * (1.0 + gate * (1.0 - sigmoid)))).astype(
            jnp.bfloat16
        )
        grad_up = (grad_hidden * swish).astype(jnp.bfloat16)
        grad_feed_in = contract_last(grad_gate, back_gate) + contract_last(grad_up, back_up)
        grad_feed_gain = grad_feed_gain + jnp.sum(grad_feed_in * feed_normed, axis=0)
        grad_residual = grad_out.astype(jnp.float32) + norm_back(
            residual, grad_feed_in * back_gain_feed.astype(jnp.float32)
        )
        grad_proj = grad_residual.astype(jnp.bfloat16)
        grad_mixed = (
            contract_last(grad_proj, back_out).astype(jnp.bfloat16).reshape(tokens, HK, groups, HD)
        )
        delta = jnp.transpose(jnp.sum(grad_mixed.astype(jnp.float32) * mixed, axis=-1), (1, 2, 0))

        def add_grads(state, block, offset):
            grad_query, grad_keys, grad_values = state
            keys, values_block, key_seg = block
            masked, visible, shaped = key_scores(keys, key_seg, offset)
            rows = keys.shape[0]
            probs = jnp.exp(masked - lse[..., None])
            probs_low = probs.astype(jnp.bfloat16)
            value_heads = values_block.reshape(rows, HK, HD)
            grad_probs = jnp.einsum(
                "qkgd,skd->kgqs", grad_mixed, value_heads, preferred_element_type=jnp.float32
            )
            grad_scores = (probs * (grad_probs - delta[..., None])).astype(jnp.bfloat16)
            grad_query = (
                grad_query
                + jnp.einsum(
                    "kgqs,skd->qkgd", grad_scores, shaped, preferred_element_type=jnp.float32
                )
                * scale
            )
            key_part = (
                jnp.einsum(
                    "kgqs,qkgd->skd", grad_scores, grouped, preferred_element_type=jnp.float32
                )
                * scale
            )
            value_part = jnp.einsum(
                "kgqs,qkgd->skd", probs_low, grad_mixed, preferred_element_type=jnp.float32
            )
            old_keys = lax.dynamic_slice_in_dim(grad_keys, offset, rows, 0)
            grad_keys = lax.dynamic_update_slice_in_dim(
                grad_keys, old_keys + key_part.reshape(rows, HK * HD), offset, 0
            )
            old_values = lax.dynamic_slice_in_dim(grad_values, offset, rows, 0)
            grad_values = lax.dynamic_update_slice_in_dim(
                grad_values, old_values + value_part.reshape(rows, HK * HD), offset, 0
            )
            return (grad_query, grad_keys, grad_values)

        back_state = (
            jnp.zeros((tokens, HK, groups, HD), jnp.float32),
            jnp.zeros((length, HK * HD), jnp.float32),
            jnp.zeros((length, HK * HD), jnp.float32),
        )
        grad_query, grad_keys_all, grad_values_all = fold_with(
            add_grads,
            back_state,
            (
                lax.all_gather(keys_flat, "ctx", axis=0, tiled=True),
                lax.all_gather(values, "ctx", axis=0, tiled=True),
                lax.all_gather(query_seg, "ctx", axis=0, tiled=True),
            ),
        )
        grad_keys_own, grad_values_own = (
            lax.psum_scatter(
                grad_keys_all.astype(jnp.bfloat16), "ctx", scatter_dimension=0, tiled=True
            ).astype(jnp.float32),
            lax.psum_scatter(
                grad_values_all.astype(jnp.bfloat16), "ctx", scatter_dimension=0, tiled=True
            ).astype(jnp.float32),
        )
        turned_query = rotate_back(grad_query.reshape(tokens, HQ, HD), cosine, sine)
        grad_query_gain = grad_query_gain + jnp.sum(turned_query * query_norm, axis=(0, 1))
        grad_query_low = (
            norm_back(query_heads, turned_query * back_gain_query.astype(jnp.float32))
            .reshape(tokens, HQ * HD)
            .astype(jnp.bfloat16)
        )
        turned_key = rotate_back(grad_keys_own.reshape(tokens, HK, HD), cosine, sine)
        grad_key_gain = grad_key_gain + jnp.sum(turned_key * key_norm, axis=(0, 1))
        grad_key_low = (
            norm_back(key_heads, turned_key * back_gain_key.astype(jnp.float32))
            .reshape(tokens, HK * HD)
            .astype(jnp.bfloat16)
        )
        grad_value_low = grad_values_own.astype(jnp.bfloat16)
        grad_scaled_in = (
            contract_last(grad_query_low, back_query)
            + contract_last(grad_key_low, back_key)
            + contract_last(grad_value_low, back_value)
        )
        grad_attention_gain = grad_attention_gain + jnp.sum(grad_scaled_in * normed, axis=0)
        input_grads.append(
            grad_residual + norm_back(hidden, grad_scaled_in * back_gain_in.astype(jnp.float32))
        )
        stored.append(
            (
                scaled_in,
                grad_query_low,
                grad_key_low,
                grad_value_low,
                ff_in,
                grad_gate,
                grad_up,
                grad_proj,
                mixed_low,
                grad_out,
                hidden_low,
            )
        )
    columns = [jnp.concatenate([entry[index] for entry in stored], axis=0) for index in range(11)]
    (
        all_in,
        all_query,
        all_key,
        all_value,
        all_feed,
        all_gate,
        all_up,
        all_proj,
        all_mixed,
        all_out,
        all_hidden,
    ) = columns
    rows = query_weight.shape[0]
    head_rows = query_gain.shape[0]
    count = lax.axis_size(("dp", "ctx")) * rows
    row_ids = jnp.arange(count, dtype=jnp.int32)
    local = row_ids % rows
    place = jnp.clip(row_ids // rows * head_rows + local, 0, HD - 1)
    owned = local < head_rows
    gains = jnp.stack(
        [
            grad_attention_gain,
            grad_feed_gain,
            jnp.where(owned, jnp.take(grad_query_gain, place), 0.0),
            jnp.where(owned, jnp.take(grad_key_gain, place), 0.0),
        ],
        axis=1,
    )
    summed = lax.psum_scatter(
        jnp.concatenate(
            [
                contract_first(all_in, all_query),
                contract_first(all_in, all_key),
                contract_first(all_in, all_value),
                contract_first(all_feed, all_gate),
                contract_first(all_feed, all_up),
                contract_first(all_proj, all_mixed),
                contract_first(all_out, all_hidden),
                gains,
                jnp.zeros((count, 124), jnp.float32),
            ],
            axis=1,
        ),
        ("dp", "ctx"),
        scatter_dimension=0,
        tiled=True,
    )
    widths = [HQ * HD, HK * HD, HK * HD, FF, FF, HQ * HD, FF, 128]
    pieces = []
    edge = 0
    for width in widths:
        pieces.append(summed[:, edge : edge + width])
        edge = edge + width
    gain_block = pieces[7]
    block_out = jnp.stack(outputs)[:, None]
    input_grad = jnp.stack(input_grads)[:, None]
    return (
        block_out,
        input_grad,
        gain_block[:, 0],
        gain_block[:head_rows, 2],
        gain_block[:head_rows, 3],
        pieces[0],
        pieces[1],
        pieces[2],
        pieces[5].T,
        gain_block[:, 1],
        pieces[3],
        pieces[4],
        pieces[6].T,
    )


def solution(mesh):
    return jax.shard_map(
        on_device,
        mesh=mesh,
        in_specs=(
            P(None, "dp", "ctx", None),
            P(None, "dp", "ctx"),
            P(("dp", "ctx")),
            P(("dp", "ctx")),
            P(("dp", "ctx")),
            P(("dp", "ctx"), None),
            P(("dp", "ctx"), None),
            P(("dp", "ctx"), None),
            P(None, ("dp", "ctx")),
            P(("dp", "ctx")),
            P(("dp", "ctx"), None),
            P(("dp", "ctx"), None),
            P(None, ("dp", "ctx")),
            P(None, "dp", "ctx", None),
        ),
        out_specs=(
            P(None, "dp", "ctx", None),
            P(None, "dp", "ctx", None),
            P(("dp", "ctx")),
            P(("dp", "ctx")),
            P(("dp", "ctx")),
            P(("dp", "ctx"), None),
            P(("dp", "ctx"), None),
            P(("dp", "ctx"), None),
            P(None, ("dp", "ctx")),
            P(("dp", "ctx")),
            P(("dp", "ctx"), None),
            P(("dp", "ctx"), None),
            P(None, ("dp", "ctx")),
        ),
        check_vma=False,
    )
```

profile of v0, /device:TPU:0, one launch (start us, length us, event | category | flops | bytes accessed | tf_op | source)
XLA Modules:
  0.0 2800.4 jit_solution(5882778929059811977)
XLA Ops:
  12.1 42.1 %all-reduce.9 = (bf16[1024]{0:T(1024)(128)(2,1)S(1)}, bf16[128]{0:T(256)(128)(2,1)S(1)}, bf16[128]{0:T(256)(128)(2,1)}, bf16[1024]{0:T(1024)(128)(2,1)}) all-reduce(bf16[1024]{0:T(1024)(128)(2,1)S(1)} %dynamic-update-slice, bf16[128]{0:T(256)(128)(2,1)S(1)} %dynamic-update-slice.2, ...), channel_id=1, replica_groups=mesh['dp'=4,'ctx'=8] {'dp','ctx'}, use_global_device_ids=true, to_apply=%add | all-reduce | flops 2304 | bytes 9216
  58.4 11.9 all-gather.20.cloned.1.call-done
  70.3 2.9 convolution_convert_fusion.7
  76.1 52.6 %all-gather.24.cloned.1.call-done = bf16[1024,1024]{1,0:T(8,128)(2,1)} async-done(((bf16[32,1024]{1,0:T(8,128)(2,1)}), bf16[1024,1024]{1,0:T(8,128)(2,1)}) %all-gather.24.cloned.1.call-update) | async-done | bytes 2097168 | tf_op jit(solution)/shard_map/all_gather | solution.py:78
  128.7 4.0 copy.259
  137.0 3.3 multiply_reduce_fusion.33
  153.7 10.8 all-reduce.8
  165.3 5.2 all-gather.22.cloned.1.call-done
  172.9 39.0 %all-gather.38.cloned.1.call-done = bf16[512,1024]{1,0:T(8,128)(2,1)} async-done(((bf16[64,1024]{1,0:T(8,128)(2,1)}), bf16[512,1024]{1,0:T(8,128)(2,1)}) %all-gather.38.cloned.1.call-update) | async-done | bytes 1048592 | tf_op jit(solution)/shard_map/all_gather | solution.py:230
  214.4 39.0 %all-gather.42.cloned.1.call-done = bf16[512,1024]{1,0:T(8,128)(2,1)} async-done(((bf16[64,1024]{1,0:T(8,128)(2,1)}), bf16[512,1024]{1,0:T(8,128)(2,1)}) %all-gather.42.cloned.1.call-update) | async-done | bytes 1048592 | tf_op jit(solution)/shard_map/all_gather | solution.py:230
  253.4 2.5 copy.429
  255.9 39.0 %all-gather.46.cloned.1.call-done = bf16[512,1024]{1,0:T(8,128)(2,1)} async-done(((bf16[64,1024]{1,0:T(8,128)(2,1)}), bf16[512,1024]{1,0:T(8,128)(2,1)}) %all-gather.46.cloned.1.call-update) | async-done | bytes 1048592 | tf_op jit(solution)/shard_map/all_gather | solution.py:230
  297.3 39.2 %all-gather.26.cloned.1.call-done = bf16[512,1024]{1,0:T(8,128)(2,1)} async-done(((bf16[64,1024]{1,0:T(8,128)(2,1)}), bf16[512,1024]{1,0:T(8,128)(2,1)}) %all-gather.26.cloned.1.call-update) | async-done | bytes 1048592 | tf_op jit(solution)/shard_map/all_gather | solution.py:229
  338.8 39.4 %all-gather.40.cloned.1.call-done = bf16[512,1024]{1,0:T(8,128)(2,1)} async-done(((bf16[64,1024]{1,0:T(8,128)(2,1)}), bf16[512,1024]{1,0:T(8,128)(2,1)}) %all-gather.40.cloned.1.call-update) | async-done | bytes 1048592 | tf_op jit(solution)/shard_map/all_gather | solution.py:229
  380.4 39.4 %all-gather.44.cloned.1.call-done = bf16[512,1024]{1,0:T(8,128)(2,1)} async-done(((bf16[64,1024]{1,0:T(8,128)(2,1)}), bf16[512,1024]{1,0:T(8,128)(2,1)}) %all-gather.44.cloned.1.call-update) | async-done | bytes 1048592 | tf_op jit(solution)/shard_map/all_gather | solution.py:229
  422.1 39.2 %all-gather.48.cloned.1.call-done = bf16[512,1024]{1,0:T(8,128)(2,1)} async-done(((bf16[64,1024]{1,0:T(8,128)(2,1)}), bf16[512,1024]{1,0:T(8,128)(2,1)}) %all-gather.48.cloned.1.call-update) | async-done | bytes 1048592 | tf_op jit(solution)/shard_map/all_gather | solution.py:229
  463.6 61.7 %all-gather.28.cloned.1.call-done = bf16[1024,2048]{1,0:T(8,128)(2,1)} async-done(((bf16[32,2048]{1,0:T(8,128)(2,1)}), bf16[1024,2048]{1,0:T(8,128)(2,1)}) %all-gather.28.cloned.1.call-update) | async-done | bytes 4194320 | tf_op jit(solution)/shard_map/all_gather | solution.py:77
  525.2 6.4 copy.262
  531.6 3.8 multiply_reduce_fusion.13
  571.5 17.3 all-gather.30.cloned.1.call-done
  588.8 4.6 multiply_reduce_fusion.36
  601.2 58.6 %all-gather.34.cloned.1.call-done = bf16[1024,3072]{1,0:T(8,128)(2,1)} async-done(((bf16[32,3072]{1,0:T(8,128)(2,1)}), bf16[1024,3072]{1,0:T(8,128)(2,1)}) %all-gather.34.cloned.1.call-update) | async-done | bytes 6291472 | tf_op jit(solution)/shard_map/all_gather | solution.py:88
  659.8 4.9 fusion.305
  664.7 65.9 %all-gather.32.cloned.1.call-done = bf16[1024,3072]{1,0:T(8,128)(2,1)} async-done(((bf16[32,3072]{1,0:T(8,128)(2,1)}), bf16[1024,3072]{1,0:T(8,128)(2,1)}) %all-gather.32.cloned.1.call-update) | async-done | bytes 6291472 | tf_op jit(solution)/shard_map/all_gather | solution.py:87
  730.6 5.1 fusion.304
  740.8 60.6 %all-gather.36.cloned.1.call-done = bf16[3072,1024]{0,1:T(8,128)(2,1)} async-done(((bf16[3072,32]{0,1:T(8,128)(2,1)}), bf16[3072,1024]{0,1:T(8,128)(2,1)}) %all-gather.36.cloned.1.call-update) | async-done | bytes 6291472 | tf_op jit(solution)/shard_map/all_gather | solution.py:89
  801.4 5.4 multiply_convert_fusion.6
  807.6 5.0 fusion.312
  819.2 2.7 multiply_reduce_fusion.21
  828.5 2.7 multiply_reduce_fusion.20
  838.3 3.4 multiply_reduce_fusion.22
  848.2 2.7 fusion.5
  855.7 3.8 convolution_convert_fusion.3
  862.7 2.7 fusion.11
  870.2 3.8 convolution_convert_fusion
  877.2 2.7 fusion.2
  884.8 3.8 convolution_convert_fusion.2
  900.7 3.2 bitcast_convert_fusion.1
  906.1 3.2 bitcast_convert_fusion.3
  909.3 2.8 convolution_multiply_fusion.1
  937.2 4.4 fusion.188
  944.1 6.6 gather_fusion
  951.9 5.6 fusion.56
  957.6 6.3 fusion.24
  963.9 6.3 fusion.16
  971.8 4.5 fusion.48
  976.4 6.4 fusion.32
  991.2 58.6 %reduce-scatter.24.cloned.1.call-done = bf16[64,1024]{1,0:T(8,128)(2,1)} async-done(((bf16[512,1024]{1,0:T(8,128)(2,1)}), bf16[64,1024]{1,0:T(8,128)(2,1)}) %reduce-scatter.24.cloned.1.call-update) | async-done | bytes 131088 | tf_op jit(solution)/shard_map/reduce_scatter | solution.py:323
  1049.8 66.2 %reduce-scatter.20.cloned.1.call-done = bf16[64,1024]{1,0:T(8,128)(2,1)} async-done(((bf16[512,1024]{1,0:T(8,128)(2,1)}), bf16[64,1024]{1,0:T(8,128)(2,1)}) %reduce-scatter.20.cloned.1.call-update) | async-done | bytes 131088 | tf_op jit(solution)/shard_map/reduce_scatter | solution.py:323
  1123.0 11.3 gather_fusion.1
  1142.3 2.6 convolution_add_fusion.1
  1149.7 32.2 %reduce-scatter.32.cloned.1.call-done = bf16[64,1024]{1,0:T(8,128)(2,1)} async-done(((bf16[512,1024]{1,0:T(8,128)(2,1)}), bf16[64,1024]{1,0:T(8,128)(2,1)}) %reduce-scatter.32.cloned.1.call-update) | async-done | bytes 131088
  1181.9 2.5 convolution_add_fusion.3
  1184.4 63.8 %reduce-scatter.28.cloned.1.call-done = bf16[64,1024]{1,0:T(8,128)(2,1)} async-done(((bf16[512,1024]{1,0:T(8,128)(2,1)}), bf16[64,1024]{1,0:T(8,128)(2,1)}) %reduce-scatter.28.cloned.1.call-update) | async-done | bytes 131088
  1250.6 64.2 %reduce-scatter.30.cloned.1.call-done = bf16[64,1024]{1,0:T(8,128)(2,1)} async-done(((bf16[512,1024]{1,0:T(8,128)(2,1)}), bf16[64,1024]{1,0:T(8,128)(2,1)}) %reduce-scatter.30.cloned.1.call-update) | async-done | bytes 131088
  1317.1 64.0 %reduce-scatter.34.cloned.1.call-done = bf16[64,1024]{1,0:T(8,128)(2,1)} async-done(((bf16[512,1024]{1,0:T(8,128)(2,1)}), bf16[64,1024]{1,0:T(8,128)(2,1)}) %reduce-scatter.34.cloned.1.call-update) | async-done | bytes 131088
  1381.1 3.6 fusion.147
  1388.4 3.1 fusion.92
  1391.5 2.7 fusion.84
  1394.3 64.9 %concatenate.119 = f32[1024,15488]{1,0:T(8,128)} concatenate(f32[1024,2048]{1,0:T(8,128)} %fusion.48, f32[1024,1024]{1,0:T(8,128)} %fusion.84, f32[1024,1024]{1,0:T(8,128)} %fusion.92, f32[1024,3072]{1,0:T(8,128)} %fusion.16, f32[1024,3072]{1,0:T(8,128)} %fusion.24, f32[1024,2048]{1,0:T(8,128)} %fusion.56, f32[1024,3072]{1,0:T(8,128)} %fusion.32, f32[1024,1]{1,0:T(8,128)S(1)} %copy.339, ...), dimensions={1} | concatenate | bytes 126877696 | tf_op jit(solution)/shard_map/concatenate | solution.py:400
  1460.2 5.0 fusion.47
  1465.2 5.0 fusion.45
  1470.2 4.9 fusion.46
  1480.1 1304.5 %reduce-scatter.26.cloned.1.call-done = f32[32,15488]{1,0:T(8,128)} async-done(((f32[1024,15488]{1,0:T(8,128)}), f32[32,15488]{1,0:T(8,128)}) %reduce-scatter.26.cloned.1.call-update) | async-done | bytes 1982480 | tf_op jit(solution)/shard_map/reduce_scatter | solution.py:399
  (804 shorter events, 237.3 us)
Async XLA Ops:
  7.2 63.1 %all-gather.20.cloned.1.call-start = ((), (), s32[]{:S(2)}) async-start(), calls=%async_computation.9 | async-start | bytes 2162688 | tf_op jit(solution)/shard_map/all_gather | solution.py:79
  7.9 120.8 %all-gather.24.cloned.1.call-start = ((), (), s32[]{:S(2)}) async-start(), calls=%async_computation.11 | async-start | bytes 2162688 | tf_op jit(solution)/shard_map/all_gather | solution.py:78
  8.7 161.8 %all-gather.22.cloned.1.call-start = ((), (), s32[]{:S(2)}) async-start(), calls=%async_computation.10 | async-start | bytes 1179648 | tf_op jit(solution)/shard_map/all_gather | solution.py:230
  56.0 85.1 %copy-start.221 = (f32[64]{0:T(128)}, f32[64]{0:T(128)S(1)}, u32[]{:S(2)}) copy-start(f32[64]{0:T(128)S(1)} %get-tuple-element.628) | copy-start | bytes 772
  56.6 80.4 %copy-start.224 = (f32[64]{0:T(128)}, f32[64]{0:T(128)S(1)}, u32[]{:S(2)}) copy-start(f32[64]{0:T(128)S(1)} %get-tuple-element.634) | copy-start | bytes 772
  57.1 83.1 %copy-start.209 = (f32[64]{0:T(128)}, f32[64]{0:T(128)S(1)}, u32[]{:S(2)}) copy-start(f32[64]{0:T(128)S(1)} %get-tuple-element.712) | copy-start | bytes 772
  57.1 474.5 %copy-start.207 = (f32[64]{0:T(128)}, f32[64]{0:T(128)S(1)}, u32[]{:S(2)}) copy-start(f32[64]{0:T(128)S(1)} %get-tuple-element.632) | copy-start | bytes 772
  58.4 16.0 copy-start.98
  58.4 16.0 copy-start.100
  58.4 16.1 copy-start.103
  58.4 77.4 %copy-start.106 = (bf16[64,1024]{1,0:T(8,128)(2,1)}, bf16[64,1024]{1,0:T(8,128)(2,1)S(1)}, u32[]{:S(2)}) copy-start(bf16[64,1024]{1,0:T(8,128)(2,1)S(1)} %get-tuple-element.534) | copy-start | bytes 393220
  73.2 138.7 %all-gather.38.cloned.1.call-start = ((), (), s32[]{:S(2)}) async-start(), calls=%async_computation.18 | async-start | bytes 1179648 | tf_op jit(solution)/shard_map/all_gather | solution.py:230
  74.4 179.0 %all-gather.42.cloned.1.call-start = ((), (), s32[]{:S(2)}) async-start(), calls=%async_computation.20 | async-start | bytes 1179648 | tf_op jit(solution)/shard_map/all_gather | solution.py:230
  75.7 219.2 %all-gather.46.cloned.1.call-start = ((), (), s32[]{:S(2)}) async-start(), calls=%async_computation.22 | async-start | bytes 1179648 | tf_op jit(solution)/shard_map/all_gather | solution.py:230
  76.0 67.4 %copy-start.227 = (f32[128]{0:T(128)}, f32[128]{0:T(128)S(1)}, u32[]{:S(2)}) copy-start(f32[128]{0:T(128)S(1)} %convert_element_type.471) | copy-start | bytes 1540
  76.1 468.2 %copy-start.138 = (f32[64,128]{1,0:T(8,128)}, f32[64,128]{1,0:T(8,128)S(1)}, u32[]{:S(2)}) copy-start(f32[64,128]{1,0:T(8,128)S(1)} %get-tuple-element.716) | copy-start | bytes 98308
  76.1 468.2 %copy-start.163 = (f32[64,128]{1,0:T(8,128)}, f32[64,128]{1,0:T(8,128)S(1)}, u32[]{:S(2)}) copy-start(f32[64,128]{1,0:T(8,128)S(1)} %get-tuple-element.717) | copy-start | bytes 98308
  135.2 8.2 copy-start.59
  142.0 194.5 %all-gather.26.cloned.1.call-start = ((), (), s32[]{:S(2)}) async-start(), calls=%async_computation.12 | async-start | bytes 1179648 | tf_op jit(solution)/shard_map/all_gather | solution.py:229
  145.7 8.0 copy-start.252
  145.7 8.0 copy-start.237
  146.4 231.8 %all-gather.40.cloned.1.call-start = ((), (), s32[]{:S(2)}) async-start(), calls=%async_computation.19 | async-start | bytes 1179648 | tf_op jit(solution)/shard_map/all_gather | solution.py:229
  147.1 272.6 %all-gather.44.cloned.1.call-start = ((), (), s32[]{:S(2)}) async-start(), calls=%async_computation.21 | async-start | bytes 1179648 | tf_op jit(solution)/shard_map/all_gather | solution.py:229
  147.9 313.4 %all-gather.48.cloned.1.call-start = ((), (), s32[]{:S(2)}) async-start(), calls=%async_computation.23 | async-start | bytes 1179648 | tf_op jit(solution)/shard_map/all_gather | solution.py:229
  148.7 376.6 %all-gather.28.cloned.1.call-start = ((), (), s32[]{:S(2)}) async-start(), calls=%async_computation.13 | async-start | bytes 4325376 | tf_op jit(solution)/shard_map/all_gather | solution.py:77
  149.4 439.4 %all-gather.30.cloned.1.call-start = ((), (), s32[]{:S(2)}) async-start(), calls=%async_computation.14 | async-start | bytes 4325376 | tf_op jit(solution)/shard_map/all_gather | solution.py:80
  150.0 509.8 %all-gather.34.cloned.1.call-start = ((), (), s32[]{:S(2)}) async-start(), calls=%async_computation.16 | async-start | bytes 6488064 | tf_op jit(solution)/shard_map/all_gather | solution.py:88
  150.7 579.9 %all-gather.32.cloned.1.call-start = ((), (), s32[]{:S(2)}) async-start(), calls=%async_computation.15 | async-start | bytes 6488064 | tf_op jit(solution)/shard_map/all_gather | solution.py:87
  151.3 650.1 %all-gather.36.cloned.1.call-start = ((), (), s32[]{:S(2)}) async-start(), calls=%async_computation.17 | async-start | bytes 6488064 | tf_op jit(solution)/shard_map/all_gather | solution.py:89
  151.9 839.3 %reduce-scatter.22.cloned.1.call-start = ((), (), s32[]{:S(2)}) async-start(), calls=%async_computation.26 | async-start | bytes 1179648 | tf_op jit(solution)/shard_map/reduce_scatter | solution.py:323
  153.7 388.4 %copy-start.218 = (f32[128]{0:T(128)}, f32[128]{0:T(128)S(1)}, u32[]{:S(2)}) copy-start(f32[128]{0:T(128)S(1)} %convert_element_type.474) | copy-start | bytes 1540
  550.6 38.2 %copy-start.114 = (bf16[64,2048]{1,0:T(8,128)(2,1)}, bf16[64,2048]{1,0:T(8,128)(2,1)S(1)}, u32[]{:S(2)}) copy-start(bf16[64,2048]{1,0:T(8,128)(2,1)S(1)} %convert_element_type.494) | copy-start | bytes 786436
  601.2 129.4 %copy-start.94 = (bf16[64,1024]{1,0:T(8,128)(2,1)}, bf16[64,1024]{1,0:T(8,128)(2,1)S(1)}, u32[]{:S(2)}) copy-start(bf16[64,1024]{1,0:T(8,128)(2,1)S(1)} %get-tuple-element.619) | copy-start | bytes 393220
  801.4 11.1 copy-start.35
  801.4 11.1 copy-start.109
  801.4 11.1 copy-start.110
  801.4 13.3 slice-start.4
  806.8 10.0 copy-start.68
  807.6 9.2 slice-start.2
  855.7 135.5 %reduce-scatter.18.cloned.1.call-start = ((), (), s32[]{:S(2)}) async-start(), calls=%async_computation.24 | async-start | bytes 1179648 | tf_op jit(solution)/shard_map/reduce_scatter | solution.py:323
  870.2 179.6 %reduce-scatter.24.cloned.1.call-start = ((), (), s32[]{:S(2)}) async-start(), calls=%async_computation.27 | async-start | bytes 1179648 | tf_op jit(solution)/shard_map/reduce_scatter | solution.py:323
  884.7 231.3 %reduce-scatter.20.cloned.1.call-start = ((), (), s32[]{:S(2)}) async-start(), calls=%async_computation.25 | async-start | bytes 1179648 | tf_op jit(solution)/shard_map/reduce_scatter | solution.py:323
  898.7 283.2 %reduce-scatter.32.cloned.1.call-start = ((), (), s32[]{:S(2)}) async-start(), calls=%async_computation.31 | async-start | bytes 1179648
  898.8 45.2 %copy-start.204 = (s32[1024]{0:T(1024)}, s32[1024]{0:T(1024)S(1)}, u32[]{:S(2)}) copy-start(s32[1024]{0:T(1024)S(1)} %broadcast_clamp_fusion) | copy-start | bytes 12292
  909.3 338.9 %reduce-scatter.28.cloned.1.call-start = ((), (), s32[]{:S(2)}) async-start(), calls=%async_computation.29 | async-start | bytes 1179648
  924.9 389.8 %reduce-scatter.30.cloned.1.call-start = ((), (), s32[]{:S(2)}) async-start(), calls=%async_computation.30 | async-start | bytes 1179648
  937.1 444.0 %reduce-scatter.34.cloned.1.call-start = ((), (), s32[]{:S(2)}) async-start(), calls=%async_computation.32 | async-start | bytes 1179648
  944.0 7.7 copy-start.206
  944.0 7.7 copy-start.115
  944.0 7.7 copy-start.117
  951.8 18.8 copy-start.192
  970.3 1814.3 %reduce-scatter.26.cloned.1.call-start = ((), (), s32[]{:S(2)}) async-start(), calls=%async_computation.28 | async-start | bytes 65421312 | tf_op jit(solution)/shard_map/reduce_scatter | solution.py:399
  989.1 127.0 %copy-start.165 = (f32[64,128]{1,0:T(8,128)S(1)}, f32[64,128]{1,0:T(8,128)}, u32[]{:S(2)}) copy-start(f32[64,128]{1,0:T(8,128)} %copy-done.163) | copy-start | bytes 98308
  1134.3 7.9 copy-start.9
  1147.4 34.5 %copy-start.6 = (bf16[1024,1024]{1,0:T(8,128)(2,1)S(1)}, bf16[1024,1024]{1,0:T(8,128)(2,1)}, u32[]{:S(2)}) copy-start(bf16[1024,1024]{1,0:T(8,128)(2,1)} %all-gather.20.cloned.1.call-done) | copy-start | bytes 6291460
  1149.7 98.5 %copy-start.162 = (f32[64,1024]{1,0:T(8,128)S(1)}, f32[64,1024]{1,0:T(8,128)}, u32[]{:S(2)}) copy-start(f32[64,1024]{1,0:T(8,128)} %convolution_add_fusion.10) | copy-start | bytes 786436
  1184.4 196.7 %copy-start.208 = (f32[64]{0:T(128)S(1)}, f32[64]{0:T(128)}, u32[]{:S(2)}) copy-start(f32[64]{0:T(128)} %copy-done.207) | copy-start | bytes 772
  1184.4 196.7 %copy-start.211 = (f32[64]{0:T(128)S(1)}, f32[64]{0:T(128)}, u32[]{:S(2)}) copy-start(f32[64]{0:T(128)} %copy-done.209) | copy-start | bytes 772
  1184.4 196.7 %copy-start.223 = (f32[64]{0:T(128)S(1)}, f32[64]{0:T(128)}, u32[]{:S(2)}) copy-start(f32[64]{0:T(128)} %copy-done.221) | copy-start | bytes 772
  1317.1 71.2 %copy-start.102 = (bf16[64,1024]{1,0:T(8,128)(2,1)S(1)}, bf16[64,1024]{1,0:T(8,128)(2,1)}, u32[]{:S(2)}) copy-start(bf16[64,1024]{1,0:T(8,128)(2,1)} %copy-done.100) | copy-start | bytes 393220
  1317.1 71.2 %copy-start.105 = (bf16[64,1024]{1,0:T(8,128)(2,1)S(1)}, bf16[64,1024]{1,0:T(8,128)(2,1)}, u32[]{:S(2)}) copy-start(bf16[64,1024]{1,0:T(8,128)(2,1)} %copy-done.103) | copy-start | bytes 393220
  1317.1 71.2 %copy-start.108 = (bf16[64,1024]{1,0:T(8,128)(2,1)S(1)}, bf16[64,1024]{1,0:T(8,128)(2,1)}, u32[]{:S(2)}) copy-start(bf16[64,1024]{1,0:T(8,128)(2,1)} %copy-done.106) | copy-start | bytes 393220
  1460.2 14.9 slice-start
  1465.2 9.9 slice-start.1
  (220 other events, 699.0 us)
Sparse Core Ops, SparseCore 0:
  11.0 59.2 all-gather.19
  73.3 55.3 all-gather.23
  131.4 38.9 all-gather.21
  173.0 38.8 all-gather.37
  214.5 38.8 all-gather.41
  255.9 38.8 all-gather.45
  297.6 38.8 all-gather.25
  339.2 38.8 all-gather.39
  380.9 38.8 all-gather.43
  422.3 38.8 all-gather.47
  464.4 60.8 all-gather.27
  528.2 60.6 all-gather.29
  591.7 68.0 all-gather.33
  662.6 67.9 all-gather.31
  733.4 68.0 all-gather.35
  855.8 61.9 reduce-scatter.21
  921.5 62.5 reduce-scatter.17
  987.3 62.4 reduce-scatter.23
  1053.6 62.4 reduce-scatter.19
  1119.3 62.4 reduce-scatter.31
  1185.7 62.4 reduce-scatter.27
  1252.2 62.5 reduce-scatter.29
  1318.5 62.5 reduce-scatter.33
  1459.3 1325.2 reduce-scatter.25
where the time goes:
time: 2810 us; the launch traced here: 2800 us
  waiting for transfers between devices  2270 us (81%)
  matrix products  220 us (8%)
  local copies, waits for them, and re-layouts  189 us (7%)
  blocking collectives  52.9 us (2%)
  other arithmetic  52.5 us (2%)
    reduce_scatter x1, waiting for transfers between devices, on_device(): lax.psum_scatter(jnp.concatenate([contract_first(all_in, all_query), cont...  1300 us
    unnamed x28, waiting for transfers between devices  229 us
    all_gather x4, waiting for transfers between devices, on_device(): lax.all_gather(keys_flat, 'ctx', axis=0, tiled=True)  157 us
    reduce_scatter x4, waiting for transfers between devices, on_device(): lax.psum_scatter(grad_keys_all.astype(jnp.bfloat16), 'ctx', scatter_dimen...  125 us
    all_gather x4, waiting for transfers between devices, on_device(): lax.all_gather(values, 'ctx', axis=0, tiled=True)  122 us
    dot_general x28, matrix products, contract_last(): lax.dot_general(left, right, (((1,), (1,)), ((), ())), preferred_element_...  73.8 us
    all_gather x1, waiting for transfers between devices, fetch_feedforward(): lax.all_gather(gate_weight, ('dp', 'ctx'), axis=0, tiled=True)  65.9 us
    concatenate x1, local copies, waits for them, and re-layouts, on_device(): jnp.concatenate([contract_first(all_in, all_query), contract_first(all_in...  64.9 us
  transfers between devices with their start and end apart: 24, of which 22 were waited for; matrix products, arithmetic and copies ran while one was open for 11% of the time, Pallas kernels for 0%

commit v1 on v0

--- a/solution.py
+++ b/solution.py
@@ -1,6 +1,11 @@
+import functools
+import types
+
 import jax
 import jax.numpy as jnp
 from jax import lax
+from jax.experimental import pallas as pl
+from jax.experimental.pallas import tpu as pltpu
 from jax.sharding import PartitionSpec as P
 
 D = 1024
@@ -10,10 +15,13 @@
 FF = 3072
 MB = 4
 
-
 NORM_EPS = 1e-06
 ROPE_BASE = 1000000.0
 MASKED = -1e30
+SCALE = HD ** (-0.5)
+BF = jnp.bfloat16
+F32 = jnp.float32
+MESH = pl.DeviceIdType.MESH
 
 
 def normalize(value):
@@ -27,10 +35,958 @@
     )
 
 
+def rope_angles(first, count):
+    positions = (first + jnp.arange(count, dtype=jnp.int32)).astype(F32)
+    frequency = ROPE_BASE ** (-(jnp.arange(HD // 2, dtype=F32) * 2.0) / HD)
+    return positions[:, None] * frequency[None, :]
+
+
+WIDTHS = dict(
+    e=128,
+    k=HK * HD // 2,
+    v=HK * HD // 2,
+    q=HQ * HD // 2,
+    o=HQ * HD // 2,
+    g=FF // 2,
+    u=FF // 2,
+    d=FF // 2,
+)
+ORDER = tuple(WIDTHS)
+HALF_HQ, HALF_HK = HQ // 2, HK // 2
+
+
+def split_columns(name):
+    width = WIDTHS[name]
+    first = max(128, width // 2)
+    return first, width - first
+
+
+def dot(left, right):
+    return jnp.dot(left, right, preferred_element_type=F32)
+
+
+def dot_nt(left, right):
+    return lax.dot_general(left, right, (((1,), (1,)), ((), ())), preferred_element_type=F32)
+
+
+def dot_tn(left, right):
+    return lax.dot_general(left, right, (((0,), (0,)), ((), ())), preferred_element_type=F32)
+
+
+class Semaphores:
+    def __init__(self):
+        self.count = 0
+
+    def take(self, number=1):
+        first = self.count
+        self.count += number
+        return first
+
+
+def layer_kernel(names, tokens, *refs):
+    at = types.SimpleNamespace(**dict(zip(names, refs)))
+    sends, recvs = at.sends, at.recvs
+    places = Semaphores()
+    dp, ctx = lax.axis_index("dp"), lax.axis_index("ctx")
+    x, c = lax.div(dp, 2), lax.rem(dp, 2)
+    z, y = lax.div(ctx, 2), lax.rem(ctx, 2)
+    ox, oc, oy = 1 - x, 1 - c, 1 - y
+    sibling = (2 * x + oc, ctx)
+    x_next = (2 * ox + c, ctx)
+    y_next = (dp, 2 * z + oy)
+    length = 8 * tokens
+    own_rows = 4 * tokens
+    half = length // 2
+
+    def z_at(step):
+        return lax.rem(z + step, 4)
+
+    def z_device(step):
+        return (dp, 2 * z_at(step) + y)
+
+    def remote(src, dst, place, device, recv_place=None):
+        return pltpu.make_async_remote_copy(
+            src_ref=src,
+            dst_ref=dst,
+            send_sem=sends.at[place],
+            recv_sem=recvs.at[place if recv_place is None else recv_place],
+            device_id=device,
+            device_id_type=MESH,
+        )
+
+    def arrived(region, place, device):
+        remote(region, region, place, device).wait_recv()
+
+    barrier = pltpu.get_barrier_semaphore()
+    me = c * 8 + ctx
+    for other in range(1, 16):
+        there = lax.rem(me + other, 16)
+        pl.semaphore_signal(
+            barrier, inc=1, device_id=(2 * x + lax.div(there, 8), lax.rem(there, 8)), device_id_type=MESH
+        )
+    pl.semaphore_signal(barrier, inc=1, device_id=x_next, device_id_type=MESH)
+    pl.semaphore_wait(barrier, 16)
+
+    weight = {n: getattr(at, "w_" + n) for n in ORDER}
+    shard = {n: getattr(at, "in_" + n) for n in ORDER}
+    s0 = {n: places.take() for n in ORDER}
+    lc = {n: places.take() for n in ORDER}
+    sz = {n: places.take(6) for n in ORDER}
+    s2 = {n: places.take(2) for n in ORDER}
+    s3 = {n: places.take(2) for n in ORDER}
+    gather_sends = {n: [] for n in ORDER}
+
+    def part(name, which):
+        if name == "e":
+            return shard[name]
+        width = WIDTHS[name]
+        return shard[name].at[:, pl.ds(pl.multiple_of(which * width, width), width)]
+
+    def local(name):
+        return pltpu.make_async_copy(part(name, c), weight[name].at[x, c, z, y], recvs.at[lc[name]])
+
+    def begin(name, copy):
+        copy.start()
+        gather_sends[name].append(copy)
+
+    def gather_core(name):
+        begin(name, remote(part(name, oc), weight[name].at[x, c, z, y], s0[name], sibling))
+        local(name).start()
+
+    def gather_z_own(name):
+        for step in (1, 2, 3):
+            begin(
+                name,
+                remote(
+                    part(name, c), weight[name].at[x, c, z, y], sz[name] + step - 1, z_device(step)
+                ),
+            )
+
+    def gather_z_sibling(name):
+        block = weight[name].at[x, oc, z, y]
+        arrived(block, s0[name], sibling)
+        for step in (1, 2, 3):
+            begin(name, remote(block, block, sz[name] + 2 + step, z_device(step)))
+
+    def gather_start(name):
+        gather_core(name)
+        gather_z_own(name)
+
+    def gather_two(name):
+        w = weight[name]
+        local(name).wait()
+        for step in (1, 2, 3):
+            source = lax.rem(z + 4 - step, 4)
+            device = (dp, 2 * source + y)
+            arrived(w.at[x, c, source, y], sz[name] + step - 1, device)
+            arrived(w.at[x, oc, source, y], sz[name] + 2 + step, device)
+        first, second = split_columns(name)
+        one = w.at[x, :, :, y, :, pl.ds(0, first)]
+        begin(name, remote(one, one, s2[name], x_next))
+        if second:
+            two = w.at[x, :, :, y, :, pl.ds(first, second)]
+            begin(name, remote(two, two, s2[name] + 1, y_next))
+
+    def gather_three(name):
+        w = weight[name]
+        first, second = split_columns(name)
+        arrived(w.at[ox, :, :, y, :, pl.ds(0, first)], s2[name], x_next)
+        one = w.at[:, :, :, y, :, pl.ds(0, first)]
+        begin(name, remote(one, one, s3[name], y_next))
+        if second:
+            arrived(w.at[x, :, :, oy, :, pl.ds(first, second)], s2[name] + 1, y_next)
+            two = w.at[x, :, :, :, :, pl.ds(first, second)]
+            begin(name, remote(two, two, s3[name] + 1, x_next))
+
+    def gather_done(name):
+        w = weight[name]
+        first, second = split_columns(name)
+        arrived(w.at[:, :, :, oy, :, pl.ds(0, first)], s3[name], y_next)
+        if second:
+            arrived(w.at[ox, :, :, :, :, pl.ds(first, second)], s3[name] + 1, x_next)
+
+    def gather_sent(name):
+        for copy in gather_sends[name]:
+            copy.wait_send()
+
+    slot = 2 * lax.rem(z, 2) + y
+    target_core = lax.div(z, 2)
+
+    class Reshard:
+        def __init__(self, source, landing):
+            self.source, self.landing = source, landing
+            self.place, self.recv, self.own = places.take(4), places.take(4), places.take()
+
+        def device(self, m):
+            return (2 * x + target_core, 2 * m + c)
+
+        def keeps(self, m):
+            return (target_core == c) & (z == m) & (y == c)
+
+        def copy(self, m):
+            return remote(
+                self.source.at[m], self.landing(target_core, slot), self.place + m, self.device(m), self.recv + slot
+            )
+
+        def keep(self, m):
+            return pltpu.make_async_copy(
+                self.source.at[m], self.landing(target_core, slot), recvs.at[self.own]
+            )
+
+        def start(self):
+            for m in range(MB):
+                pl.when(jnp.logical_not(self.keeps(m)))(lambda m=m: self.copy(m).start())
+                pl.when(self.keeps(m))(lambda m=m: self.keep(m).start())
+
+        def wait(self):
+            for j in range(4):
+                mine = (y == c) & (4 * c + j == ctx)
+                region = self.landing(c, j)
+                device = (2 * x + y, 4 * c + j)
+                pl.when(jnp.logical_not(mine))(
+                    lambda j=j, region=region, device=device: arrived(region, self.recv + j, device)
+                )
+                pl.when(mine)(
+                    lambda region=region: pltpu.make_async_copy(
+                        region, region, recvs.at[self.own]
+                    ).wait()
+                )
+
+        def sent(self):
+            for m in range(MB):
+                pl.when(jnp.logical_not(self.keeps(m)))(lambda m=m: self.copy(m).wait_send())
+
+    class Return:
+        def __init__(self, source, landing):
+            self.source, self.landing = source, landing
+            self.place, self.recv, self.own = places.take(4), places.take(4), places.take()
+
+        def keeps(self, j):
+            return (y == c) & (4 * c + j == ctx)
+
+        def copy(self, j):
+            return remote(
+                self.source.at[j], self.landing.at[z], self.place + j, (2 * x + y, 4 * c + j), self.recv + z
+            )
+
+        def keep(self, j):
+            return pltpu.make_async_copy(
+                self.source.at[j], self.landing.at[z], recvs.at[self.own]
+            )
+
+        def start(self, j):
+            pl.when(jnp.logical_not(self.keeps(j)))(lambda: self.copy(j).start())
+            pl.when(self.keeps(j))(lambda: self.keep(j).start())
+
+        def finish(self):
+            for j in range(4):
+                pl.when(jnp.logical_not(self.keeps(j)))(lambda j=j: self.copy(j).wait_send())
+                pl.when(self.keeps(j))(lambda j=j: self.keep(j).wait())
+            for m in range(MB):
+                mine = (target_core == c) & (z == m) & (y == c)
+                device = (2 * x + target_core, 2 * m + c)
+                pl.when(jnp.logical_not(mine))(
+                    lambda m=m, device=device: arrived(self.landing.at[m], self.recv + m, device)
+                )
+
+    hidden_own, cot_all, seg_all = at.hidden_own, at.cot_all, at.seg_all
+    hidden_move = Reshard(at.hidden_in, lambda core, j: hidden_own.at[j])
+    cot_move = Reshard(at.cotangent, lambda core, j: cot_all.at[4 * core + j])
+    out_move = Return(at.out_own, at.block_out)
+    grad_move = Return(at.grad_own, at.input_grad)
+    seg_place, seg_recv, seg_own = places.take(8), places.take(8), places.take()
+
+    def seg_cases():
+        for m in range(MB):
+            for core in range(2):
+                keeps = (core == c) & (z == m) & (y == c)
+                yield m, core, keeps
+
+    def seg_copy(m, core):
+        return remote(
+            at.segments.at[m], seg_all.at[ctx], seg_place + 2 * m + core, (2 * x + core, 2 * m + c), seg_recv + ctx
+        )
+
+    def seg_start():
+        for m, core, keeps in seg_cases():
+            pl.when(jnp.logical_not(keeps))(lambda m=m, core=core: seg_copy(m, core).start())
+            pl.when(keeps)(
+                lambda m=m: pltpu.make_async_copy(
+                    at.segments.at[m], seg_all.at[ctx], recvs.at[seg_own]
+                ).start()
+            )
+
+    def seg_wait():
+        for m, core, keeps in seg_cases():
+            pl.when(jnp.logical_not(keeps))(lambda m=m, core=core: seg_copy(m, core).wait_send())
+        for j in range(8):
+            mine = (y == c) & (ctx == j)
+            pl.when(jnp.logical_not(mine))(
+                lambda j=j: arrived(seg_all.at[j], seg_recv + j, (2 * x + y, j))
+            )
+            pl.when(mine)(
+                lambda j=j: pltpu.make_async_copy(
+                    seg_all.at[j], seg_all.at[j], recvs.at[seg_own]
+                ).wait()
+            )
+
+    class Swap:
+        def __init__(self, source, there, here):
+            self.place = places.take()
+            self.out = remote(source, there, self.place, sibling)
+            self.here = here
+
+        def start(self):
+            self.out.start()
+
+        def wait(self):
+            self.out.wait_send()
+            arrived(self.here, self.place, sibling)
+
+    def swap_rows(ref):
+        mine, theirs = ref.at[pl.ds(own_at, own_rows)], ref.at[pl.ds(other_at, own_rows)]
+        return Swap(mine, mine, theirs)
+
+    own_at = pl.multiple_of(c * own_rows, own_rows)
+    other_at = pl.multiple_of(oc * own_rows, own_rows)
+    partial_out, partial_in = at.partial_out, at.partial_in
+
+    def swap_partial(index):
+        landing = partial_in.at[index]
+        return Swap(partial_out.at[index % 2], landing, landing)
+
+    r1 = {n: places.take(2) for n in ORDER}
+    r2 = {n: places.take(2) for n in ORDER}
+    r3 = {n: places.take(3) for n in ORDER}
+    r4 = {n: places.take() for n in ORDER}
+    sum_sends = []
+
+    def send(copy):
+        copy.start()
+        sum_sends.append(copy)
+
+    def sum_one(name):
+        w = weight[name]
+        first, second = split_columns(name)
+        send(remote(w.at[:, :, :, oy, :, pl.ds(0, first)], getattr(at, "r1a_" + name), r1[name], y_next))
+        if second:
+            send(remote(w.at[ox, :, :, :, :, pl.ds(first, second)], getattr(at, "r1b_" + name), r1[name] + 1, x_next))
+
+    def sum_two(name):
+        w = weight[name]
+        first, second = split_columns(name)
+        arrived(getattr(at, "r1a_" + name), r1[name], y_next)
+
+        @pl.loop(0, 16)
+        def _(i):
+            xx, cc, zz = lax.div(i, 8), lax.rem(lax.div(i, 4), 2), lax.rem(i, 4)
+            w[xx, cc, zz, y, :, pl.ds(0, first)] += getattr(at, "r1a_" + name)[xx, cc, zz]
+
+        send(remote(w.at[ox, :, :, y, :, pl.ds(0, first)], getattr(at, "r2a_" + name), r2[name], x_next))
+        if second:
+            arrived(getattr(at, "r1b_" + name), r1[name] + 1, x_next)
+
+            @pl.loop(0, 16)
+            def _(i):
+                cc, zz, yy = lax.div(i, 8), lax.rem(lax.div(i, 2), 4), lax.rem(i, 2)
+                w[x, cc, zz, yy, :, pl.ds(first, second)] += getattr(at, "r1b_" + name)[cc, zz, yy]
+
+            send(remote(w.at[x, :, :, oy, :, pl.ds(first, second)], getattr(at, "r2b_" + name), r2[name] + 1, y_next))
+
+    def sum_three(name):
+        w = weight[name]
+        first, second = split_columns(name)
+        arrived(getattr(at, "r2a_" + name), r2[name], x_next)
+        if second:
+            arrived(getattr(at, "r2b_" + name), r2[name] + 1, y_next)
+
+        @pl.loop(0, 8)
+        def _(i):
+            cc, zz = lax.div(i, 4), lax.rem(i, 4)
+            w[x, cc, zz, y, :, pl.ds(0, first)] += getattr(at, "r2a_" + name)[cc, zz]
+            if second:
+                w[x, cc, zz, y, :, pl.ds(first, second)] += getattr(at, "r2b_" + name)[cc, zz]
+
+        for step in (1, 2, 3):
+            send(
+                remote(
+                    w.at[x, :, z_at(step), y], getattr(at, "r3_" + name).at[step - 1], r3[name] + step - 1, z_device(step)
+                )
+            )
+
+    def sum_four(name):
+        w, landed = weight[name], getattr(at, "r3_" + name)
+        for step in (1, 2, 3):
+            arrived(landed.at[step - 1], r3[name] + step - 1, (dp, 2 * lax.rem(z + 4 - step, 4) + y))
+
+        def total(core):
+            value = w[x, core, z, y].astype(F32)
+            for step in range(3):
+                value = value + landed[step, core].astype(F32)
+            return value
+
+        width = WIDTHS[name]
+        staged, result = getattr(at, "r4_" + name), getattr(at, "out_" + name)
+        staged[...] = total(oc)
+        if name == "e":
+            send(remote(staged, at.r5_e, r4[name], sibling))
+            result[...] = total(c)
+        else:
+            columns = pl.ds(pl.multiple_of(c * width, width), width)
+            send(remote(staged, result.at[:, columns], r4[name], sibling))
+            result[:, columns] = total(c)
+
+    def sum_done(name):
+        if name == "e":
+            arrived(at.r5_e, r4[name], sibling)
+            at.out_e[...] = at.out_e[...] + at.r5_e[...]
+        else:
+            width = WIDTHS[name]
+            columns = pl.ds(pl.multiple_of(oc * width, width), width)
+            arrived(getattr(at, "out_" + name).at[:, columns], r4[name], sibling)
+
+    gains, head_gains = at.gains, at.head_gains
+    scaled, ff_in, grad_proj = at.scaled, at.ff_in, at.grad_proj
+    residual, grad_residual = at.residual, at.grad_residual
+    acc_own = at.acc_own
+    scaled_swap, ff_swap, proj_swap = swap_rows(scaled), swap_rows(ff_in), swap_rows(grad_proj)
+    cot_swap = Swap(
+        cot_all.at[pl.ds(4 * c, 4)], cot_all.at[pl.ds(4 * c, 4)], cot_all.at[pl.ds(4 * oc, 4)]
+    )
+    partials = [swap_partial(i) for i in range(4)]
+
+    def selector():
+        row = lax.broadcasted_iota(jnp.int32, (D, HD), 0)
+        column = lax.broadcasted_iota(jnp.int32, (D, HD), 1)
+        local_row = row & 31
+        hit = ((row >> 5) * 4 + local_row == column) & (local_row < 4)
+        return jnp.where(hit, 1.0, 0.0).astype(BF)
+
+    def prepare_gains():
+        columns = weight["e"][...].reshape(D, 128).astype(F32)
+        for i in range(8):
+            gains[:, i * 128 : (i + 1) * 128] = columns[i * 128 : (i + 1) * 128].T[:8]
+        head_gains[...] = dot(gains[...].astype(BF), selector())
+
+    def prepare_mask():
+        rows = [seg_all[2 * j, 0:1] + seg_all[2 * j + 1, 0:1] for j in range(4)]
+        for i in range(4):
+            query = jnp.broadcast_to(rows[i], (128, 128)).T
+            for j in range(4):
+                place = slice(i * 128, (i + 1) * 128), slice(j * 128, (j + 1) * 128)
+                if j > i:
+                    at.bias[place] = jnp.full((128, 128), MASKED, F32)
+                    continue
+                seen = query == jnp.broadcast_to(rows[j], (128, 128))
+                if i == j:
+                    seen = seen & (
+                        lax.broadcasted_iota(jnp.int32, (128, 128), 1)
+                        <= lax.broadcasted_iota(jnp.int32, (128, 128), 0)
+                    )
+                at.bias[place] = jnp.where(seen, 0.0, MASKED)
+
+    def own_block(j):
+        return pl.ds(pl.multiple_of(c * own_rows + j * tokens, tokens), tokens)
+
+    def here_block(j):
+        return pl.ds(pl.multiple_of(j * tokens, tokens), tokens)
+
+    def scale_input():
+        @pl.loop(0, 4)
+        def _(j):
+            value = normalize(hidden_own[j].astype(F32)) * gains[0:1]
+            scaled[own_block(j)] = value.astype(BF)
+
+    def columns_of(name, t, size=256):
+        return weight[name][:, :, :, :, :, pl.ds(pl.multiple_of(t * size, size), size)].reshape(D, size)
+
+    def rows_of(name, t):
+        return weight[name][lax.div(t, 2), lax.rem(t, 2)].reshape(D // 4, WIDTHS[name])
+
+    cosine, sine = at.cosine, at.sine
+
+    def turn(value):
+        return value * cosine[...] + pltpu.roll(value, HD // 2, 1) * sine[...]
+
+    def project_heads(name, gain, kept, turned):
+        @pl.loop(0, WIDTHS[name] // 256)
+        def _(t):
+            both = dot(scaled[...], columns_of(name, t))
+            for i in range(2):
+                value = both[:, i * HD : (i + 1) * HD]
+                kept[2 * t + i] = value
+                turned[2 * t + i] = turn(normalize(value) * gain).astype(BF)
+
+    def project_values():
+        @pl.loop(0, WIDTHS["v"] // 256)
+        def _(t):
+            both = dot(scaled[...], columns_of("v", t))
+            for i in range(2):
+                at.values[2 * t + i] = both[:, i * HD : (i + 1) * HD].astype(BF)
+
+    def probabilities(head, pair, block):
+        rows = slice(block * half, (block + 1) * half)
+        seen = slice(0, (block + 1) * half)
+        scores = dot_nt(at.queries[head, rows], at.keys[pair, seen]) * SCALE + at.bias[rows, seen]
+        terms = jnp.exp(scores - jnp.max(scores, axis=-1, keepdims=True))
+        return terms * (1.0 / jnp.sum(terms, axis=-1, keepdims=True))
+
+    def attend():
+        @pl.loop(0, HALF_HQ)
+        def _(head):
+            pair = lax.div(head, 2)
+            for block in range(2):
+                seen = slice(0, (block + 1) * half)
+                low = probabilities(head, pair, block).astype(BF)
+                at.mixed[
+                    block * half : (block + 1) * half, pl.ds(pl.multiple_of(head * HD, HD), HD)
+                ] = dot(low, at.values[pair, seen]).astype(BF)
+
+    def partial_product(index, terms):
+        def rows_times(first, t):
+            return sum(dot_nt(left[pl.ds(first, own_rows)], rows_of(name, t)) for left, name in terms)
+
+        @pl.loop(0, 4)
+        def _(t):
+            columns = pl.ds(pl.multiple_of(t * (D // 4), D // 4), D // 4)
+            partial_out[index % 2, :, columns] = rows_times(other_at, t).astype(BF)
+
+        partials[index].start()
+
+        @pl.loop(0, 4)
+        def _(t):
+            columns = pl.ds(pl.multiple_of(t * (D // 4), D // 4), D // 4)
+            acc_own[:, columns] = rows_times(own_at, t)
+
+    def own_sum(index, j):
+        return acc_own[here_block(j)] + partial_in[index, here_block(j)].astype(F32)
+
+    def add_residual():
+        @pl.loop(0, 4)
+        def _(j):
+            value = hidden_own[j].astype(F32) + own_sum(0, j)
+            residual[here_block(j)] = value
+            ff_in[own_block(j)] = (normalize(value) * gains[1:2]).astype(BF)
+
+    gate_part, up_part, hidden_low = at.gate_part, at.up_part, at.hidden_low
+
+    def feed_forward():
+        @pl.loop(0, WIDTHS["g"] // 256)
+        def _(t):
+            columns = pl.ds(pl.multiple_of(t * 256, 256), 256)
+            gate = dot(ff_in[...], columns_of("g", t))
+            up = dot(ff_in[...], columns_of("u", t))
+            sigmoid = 1.0 / (1.0 + jnp.exp(-gate))
+            swish = gate * sigmoid
+            hidden_low[:, columns] = (swish * up).astype(BF)
+            up_part[:, columns] = swish.astype(BF)
+            gate_part[:, columns] = (up * sigmoid * (1.0 + gate * (1.0 - sigmoid))).astype(BF)
+
+    def write_out():
+        @pl.loop(0, 4)
+        def _(j):
+            at.out_own[j] = (residual[here_block(j)] + own_sum(1, j)).astype(BF)
+
+        for j in range(4):
+            out_move.start(j)
+
+    def cotangent_rows():
+        return cot_all[...].reshape(length, D)
+
+    def grad_hidden():
+        @pl.loop(0, WIDTHS["d"] // 256)
+        def _(t):
+            columns = pl.ds(pl.multiple_of(t * 256, 256), 256)
+            grad = dot(cotangent_rows(), columns_of("d", t))
+            gate_part[:, columns] = (grad * gate_part[:, columns].astype(F32)).astype(BF)
+            up_part[:, columns] = (grad * up_part[:, columns].astype(F32)).astype(BF)
+
+    turned_rows = at.turned_rows
+
+    def transpose_rows(load):
+        @pl.loop(0, D // 128)
+        def _(t):
+            turned_rows[pl.ds(pl.multiple_of(t * 128, 128), 128)] = load(
+                pl.ds(pl.multiple_of(t * 128, 128), 128)
+            ).T
+
+    def weight_grad(name, right, first=0):
+        gather_sent(name)
+
+        @pl.loop(0, WIDTHS[name] // 256)
+        def _(t):
+            grad = dot(turned_rows[...], right[:, pl.ds(pl.multiple_of(first + t * 256, 256), 256)])
+            weight[name][:, :, :, :, :, pl.ds(pl.multiple_of(t * 256, 256), 256)] = grad.astype(BF).reshape(
+                2, 2, 4, 2, 32, 256
+            )
+
+    grad_gains = at.grad_gains
+
+    def back_residual():
+        grad_gains[...] = jnp.zeros_like(grad_gains)
+
+        @pl.loop(0, 4)
+        def _(j):
+            value = residual[here_block(j)]
+            grad = own_sum(2, j)
+            scale = lax.rsqrt(jnp.mean(value * value, axis=-1, keepdims=True) + NORM_EPS)
+            grad_gains[1:2] += jnp.sum(grad * (value * scale), axis=0, keepdims=True)
+            total = cot_all[4 * c + j].astype(F32) + norm_back(value, grad * gains[1:2])
+            grad_residual[here_block(j)] = total
+            grad_proj[own_block(j)] = total.astype(BF)
+
+    grad_mixed = gate_part
+
+    def back_mixed():
+        @pl.loop(0, WIDTHS["o"] // 256)
+        def _(t):
+            columns = pl.ds(pl.multiple_of(t * 256, 256), 256)
+            grad_mixed[:, columns] = dot(grad_proj[...], columns_of("o", t)).astype(BF)
+
+    grad_heads, grad_values = hidden_low, at.grad_values
+    grad_head_gains = at.grad_head_gains
+
+    def turn_back(value):
+        return value * cosine[...] - pltpu.roll(value, HD // 2, 1) * sine[...]
+
+    def back_head(value, grad, row, columns):
+        scale = lax.rsqrt(jnp.mean(value * value, axis=-1, keepdims=True) + NORM_EPS)
+        turned = turn_back(grad)
+        grad_head_gains[row : row + 1] += jnp.sum(turned * (value * scale), axis=0, keepdims=True)
+        grad_heads[:, columns] = norm_back(value, turned * head_gains[row : row + 1]).astype(BF)
+
+    grad_key, grad_value, grad_query = at.grad_key, at.grad_value, at.grad_query
+
+    def back_attend():
+        grad_head_gains[...] = jnp.zeros_like(grad_head_gains)
+
+        @pl.loop(0, HALF_HK)
+        def _(pair):
+            for i in range(2):
+                head = 2 * pair + i
+                lanes = pl.ds(pl.multiple_of(head * HD, HD), HD)
+                for block in (1, 0):
+                    rows = slice(block * half, (block + 1) * half)
+                    seen = slice(0, (block + 1) * half)
+                    probs = probabilities(head, pair, block)
+                    grad_out = grad_mixed[rows, lanes]
+                    grad_probs = dot_nt(grad_out, at.values[pair, seen])
+                    delta = jnp.sum(probs * grad_probs, axis=-1, keepdims=True)
+                    grad_scores = (probs * (grad_probs - delta)).astype(BF)
+                    grad_query[rows] = dot(grad_scores, at.keys[pair, seen]) * SCALE
+                    key_part = dot_tn(grad_scores, at.queries[head, rows]) * SCALE
+                    value_part = dot_tn(probs.astype(BF), grad_out)
+                    if i == 0 and block == 1:
+                        grad_key[...] = key_part
+                        grad_value[...] = value_part
+                    else:
+                        grad_key[seen] += key_part
+                        grad_value[seen] += value_part
+                back_head(at.query_acc[head], grad_query[...], 2, lanes)
+            back_head(
+                at.key_acc[pair],
+                grad_key[...],
+                3,
+                pl.ds(pl.multiple_of(WIDTHS["q"] + pair * HD, HD), HD),
+            )
+            grad_values[:, pl.ds(pl.multiple_of(pair * HD, HD), HD)] = grad_value[...].astype(BF)
+
+    def back_input():
+        @pl.loop(0, 4)
+        def _(j):
+            value = hidden_own[j].astype(F32)
+            grad = own_sum(3, j)
+            scale = lax.rsqrt(jnp.mean(value * value, axis=-1, keepdims=True) + NORM_EPS)
+            grad_gains[0:1] += jnp.sum(grad * (value * scale), axis=0, keepdims=True)
+            at.grad_own[j] = (
+                grad_residual[here_block(j)] + norm_back(value, grad * gains[0:1])
+            ).astype(BF)
+
+        for j in range(4):
+            grad_move.start(j)
+
+    def gain_grads():
+        gather_sent("e")
+        grad_gains[...] += dot_nt(grad_head_gains[...].astype(BF), selector())
+        for i in range(8):
+            block = jnp.concatenate(
+                [grad_gains[:, i * 128 : (i + 1) * 128], jnp.zeros((120, 128), F32)], axis=0
+            ).T
+            weight["e"][i // 4, (i // 2) % 2, 2 * (i % 2) : 2 * (i % 2) + 2] = block.astype(BF).reshape(2, 2, 32, 128)
+
+    for name in ("e", "k", "v"):
+        gather_start(name)
+    seg_start()
+    hidden_move.start()
+    for name in ("q", "o"):
+        gather_start(name)
+    for name in ("e", "k", "v"):
+        gather_z_sibling(name)
+    gather_two("e")
+    gather_two("k")
+    gather_three("e")
+    gather_z_sibling("q")
+    gather_two("v")
+    gather_three("k")
+    gather_done("e")
+    prepare_gains()
+    seg_wait()
+    prepare_mask()
+    hidden_move.wait()
+    scale_input()
+    scaled_swap.start()
+    gather_start("g")
+    gather_z_sibling("o")
+    gather_two("q")
+    gather_three("v")
+    cot_move.start()
+    gather_start("u")
+    gather_z_sibling("g")
+    gather_done("k")
+    scaled_swap.wait()
+    project_heads("k", head_gains[3:4], at.key_acc, at.keys)
+    gather_two("o")
+    gather_three("q")
+    gather_start("d")
+    gather_z_sibling("u")
+    gather_done("v")
+    project_values()
+    gather_two("g")
+    gather_three("o")
+    gather_z_sibling("d")
+    gather_done("q")
+    project_heads("q", head_gains[2:3], at.query_acc, at.queries)
+    cot_move.wait()
+    cot_swap.start()
+    gather_two("u")
+    gather_three("g")
+    attend()
+    gather_two("d")
+    gather_three("u")
+    gather_done("o")
+    partial_product(0, [(at.mixed, "o")])
+    partials[0].wait()
+    add_residual()
+    ff_swap.start()
+    gather_done("g")
+    gather_done("u")
+    gather_three("d")
+    ff_swap.wait()
+    feed_forward()
+    cot_swap.wait()
+    transpose_rows(lambda columns: cot_all[:, :, columns].reshape(length, 128))
+    gather_done("d")
+
+    partial_product(1, [(hidden_low, "d")])
+    grad_hidden()
+    weight_grad("d", hidden_low)
+    sum_one("d")
+    partials[1].wait()
+    write_out()
+    partial_product(2, [(gate_part, "g"), (up_part, "u")])
+    transpose_rows(lambda columns: ff_in[:, columns])
+    weight_grad("g", gate_part)
+    sum_one("g")
+    weight_grad("u", up_part)
+    sum_one("u")
+    partials[2].wait()
+    back_residual()
+    proj_swap.start()
+    sum_two("d")
+    proj_swap.wait()
+    back_mixed()
+    transpose_rows(lambda columns: grad_proj[:, columns])
+    weight_grad("o", at.mixed)
+    sum_one("o")
+    back_attend()
+    sum_three("d")
+    sum_two("g")
+    partial_product(3, [(grad_heads.at[:, pl.ds(0, WIDTHS["q"])], "q"),
+                        (grad_heads.at[:, pl.ds(WIDTHS["q"], WIDTHS["k"])], "k"),
+                        (grad_values, "v")])
+    transpose_rows(lambda columns: scaled[:, columns])
+    weight_grad("q", grad_heads)
+    sum_one("q")
+    weight_grad("k", grad_heads, WIDTHS["q"])
+    sum_one("k")
+    weight_grad("v", grad_values)
+    sum_one("v")
+    partials[3].wait()
+    back_input()
+    gain_grads()
+    sum_one("e")
+    sum_three("g")
+    sum_two("u")
+    sum_four("d")
+    sum_three("u")
+    sum_two("o")
+    sum_four("g")
+    sum_three("o")
+    sum_two("q")
+    sum_four("u")
+    sum_three("q")
+    sum_two("k")
+    sum_four("o")
+    sum_three("k")
+    sum_two("v")
+    sum_two("e")
+    sum_three("v")
+    sum_three("e")
+    for name in ("q", "k", "v", "e"):
+        sum_four(name)
+    for name in ("d", "g", "u", "o", "q", "k", "v", "e"):
+        sum_done(name)
+    for copy in sum_sends:
+        copy.wait_send()
+    hidden_move.sent()
+    cot_move.sent()
+    out_move.finish()
+    grad_move.finish()
+    assert places.count <= SEMAPHORES, places.count
+
+
+SEMAPHORES = 256
+
+
+def fused(
+    hidden_in,
+    segments,
+    attention_gain,
+    query_gain,
+    key_gain,
+    query_weight,
+    key_weight,
+    value_weight,
+    out_weight,
+    feedforward_gain,
+    gate_weight,
+    up_weight,
+    down_weight,
+    cotangent,
+):
+    tokens = hidden_in.shape[2]
+    length = 8 * tokens
+    rows = query_weight.shape[0]
+    odd = lax.rem(lax.axis_index("ctx"), 2)
+    numbers = segments[:, 0].astype(F32)
+    blank = jnp.zeros_like(numbers)
+    numbers = jnp.where(
+        odd == 0, jnp.concatenate([numbers, blank], axis=1), jnp.concatenate([blank, numbers], axis=1)
+    )
+    numbers = jnp.broadcast_to(numbers[:, None], (MB, 8, 2 * tokens))
+
+    def column(gain):
+        return jnp.pad(gain, (0, rows - gain.shape[0]))
+
+    extra = jnp.stack(
+        [attention_gain, feedforward_gain, column(query_gain), column(key_gain)], axis=1
+    )
+    extra = jnp.pad(extra, ((0, 0), (0, 124)))
+    angles = rope_angles(0, length)
+    cosine = jnp.concatenate([jnp.cos(angles), jnp.cos(angles)], axis=-1)
+    sine = jnp.concatenate([-jnp.sin(angles), jnp.sin(angles)], axis=-1)
+
+    vmem, anywhere = pl.BlockSpec(memory_space=pltpu.VMEM), pl.BlockSpec(memory_space=pl.ANY)
+    inputs = dict(
+        hidden_in=(hidden_in[:, 0], anywhere),
+        cotangent=(cotangent[:, 0], anywhere),
+        segments=(numbers, vmem),
+        cosine=(cosine, vmem),
+        sine=(sine, vmem),
+        in_e=(extra, anywhere),
+        in_k=(key_weight, anywhere),
+        in_v=(value_weight, anywhere),
+        in_q=(query_weight, anywhere),
+        in_o=(out_weight.T, anywhere),
+        in_g=(gate_weight, anywhere),
+        in_u=(up_weight, anywhere),
+        in_d=(down_weight.T, anywhere),
+    )
+    block = (MB, tokens, D)
+    outputs = dict(block_out=(block, BF, anywhere), input_grad=(block, BF, anywhere))
+    for name, width in WIDTHS.items():
+        outputs["out_" + name] = ((rows, width if name == "e" else 2 * width), F32, vmem)
+    own = 4 * tokens
+    scratch = dict(
+        hidden_own=((4, tokens, D), BF),
+        cot_all=((8, tokens, D), BF),
+        seg_all=((8, 8, 2 * tokens), F32),
+        gains=((8, D), F32),
+        head_gains=((8, HD), F32),
+        grad_gains=((8, D), F32),
+        grad_head_gains=((8, HD), F32),
+        bias=((length, length), F32),
+        scaled=((length, D), BF),
+        query_acc=((HALF_HQ, length, HD), F32),
+        key_acc=((HALF_HK, length, HD), F32),
+        queries=((HALF_HQ, length, HD), BF),
+        keys=((HALF_HK, length, HD), BF),
+        values=((HALF_HK, length, HD), BF),
+        mixed=((length, HALF_HQ * HD), BF),
+        acc_own=((own, D), F32),
+        partial_out=((2, own, D), BF),
+        partial_in=((4, own, D), BF),
+        residual=((own, D), F32),
+        grad_residual=((own, D), F32),
+        ff_in=((length, D), BF),
+        gate_part=((length, FF // 2), BF),
+        up_part=((length, FF // 2), BF),
+        hidden_low=((length, FF // 2), BF),
+        grad_proj=((length, D), BF),
+        grad_values=((length, HALF_HK * HD), BF),
+        grad_key=((length, HD), F32),
+        grad_value=((length, HD), F32),
+        grad_query=((length, HD), F32),
+        turned_rows=((D, length), BF),
+        out_own=((4, tokens, D), BF),
+        grad_own=((4, tokens, D), BF),
+        r5_e=((rows, 128), F32),
+    )
+    for name, width in WIDTHS.items():
+        first, second = split_columns(name)
+        scratch["w_" + name] = ((2, 2, 4, 2, rows, width), BF)
+        scratch["r1a_" + name] = ((2, 2, 4, rows, first), BF)
+        scratch["r2a_" + name] = ((2, 4, rows, first), BF)
+        if second:
+            scratch["r1b_" + name] = ((2, 4, 2, rows, second), BF)
+            scratch["r2b_" + name] = ((2, 4, rows, second), BF)
+        scratch["r3_" + name] = ((3, 2, rows, width), BF)
+        scratch["r4_" + name] = ((rows, width), F32)
+    names = (*inputs, *outputs, *scratch, "sends", "recvs")
+    results = pl.pallas_call(
+        functools.partial(layer_kernel, names, tokens),
+        out_shape=[jax.ShapeDtypeStruct(shape, dtype) for shape, dtype, _ in outputs.values()],
+        in_specs=[spec for _, spec in inputs.values()],
+        out_specs=[spec for _, _, spec in outputs.values()],
+        scratch_shapes=[pltpu.VMEM(shape, dtype) for shape, dtype in scratch.values()]
+        + [pltpu.SemaphoreType.DMA((SEMAPHORES,))] * 2,
+        compiler_params=pltpu.CompilerParams(
+            collective_id=0, has_side_effects=True, vmem_limit_bytes=64 * 2**20 - 2**16
+        ),
+        name="layer",
+    )(*(value for value, _ in inputs.values()))
+    got = types.SimpleNamespace(**dict(zip(outputs, results)))
+    gain_grads = got.out_e
+    heads = query_gain.shape[0]
+    return (
+        got.block_out[:, None],
+        got.input_grad.astype(F32)[:, None],
+        gain_grads[:, 0],
+        gain_grads[:heads, 2],
+        gain_grads[:heads, 3],
+        got.out_q,
+        got.out_k,
+        got.out_v,
+        got.out_o.T,
+        gain_grads[:, 1],
+        got.out_g,
+        got.out_u,
+        got.out_d.T,
+    )
+
+
 def rope_tables(first, count):
-    positions = (first + jnp.arange(count, dtype=jnp.int32)).astype(jnp.float32)
-    frequency = ROPE_BASE ** (-(jnp.arange(HD // 2, dtype=jnp.float32) * 2.0) / HD)
-    angles = positions[:, None] * frequency[None, :]
+    angles = rope_angles(first, count)
     cosine = jnp.concatenate([jnp.cos(angles), jnp.cos(angles)], axis=-1)
     sine = jnp.concatenate([jnp.sin(angles), jnp.sin(angles)], axis=-1)
     return (cosine[:, None, :], sine[:, None, :])
@@ -65,29 +1021,6 @@
     while rows % size:
         size -= 1
     return size
-
-
-def fetch_attention(
-    attention_gain, query_gain, key_gain, query_weight, key_weight, value_weight, out_weight
-):
-    return (
-        lax.all_gather(attention_gain, ("dp", "ctx"), axis=0, tiled=True),
-        lax.all_gather(query_gain, ("dp", "ctx"), axis=0, tiled=True),
-        lax.all_gather(key_gain, ("dp", "ctx"), axis=0, tiled=True),
-        lax.all_gather(query_weight, ("dp", "ctx"), axis=0, tiled=True),
-        lax.all_gather(key_weight, ("dp", "ctx"), axis=0, tiled=True),
-        lax.all_gather(value_weight, ("dp", "ctx"), axis=0, tiled=True),
-        lax.all_gather(out_weight, ("dp", "ctx"), axis=1, tiled=True),
-    )
-
-
-def fetch_feedforward(feedforward_gain, gate_weight, up_weight, down_weight):
-    return (
-        lax.all_gather(feedforward_gain, ("dp", "ctx"), axis=0, tiled=True),
-        lax.all_gather(gate_weight, ("dp", "ctx"), axis=0, tiled=True),
-        lax.all_gather(up_weight, ("dp", "ctx"), axis=0, tiled=True),
-        lax.all_gather(down_weight, ("dp", "ctx"), axis=1, tiled=True),
-    )
 
 
 def over_blocks(state, pieces, update):
@@ -107,7 +1040,7 @@
     return final
 
 
-def on_device(
+def general(
     hidden_in,
     segments,
     attention_gain,
@@ -130,16 +1063,26 @@
     length = lax.axis_size("ctx") * tokens
     query_pos = first + jnp.arange(tokens, dtype=jnp.int32)
     cosine, sine = rope_tables(first, tokens)
-    attention_shards = (
-        attention_gain,
-        query_gain,
-        key_gain,
+    sources = (
         query_weight,
         key_weight,
         value_weight,
-        out_weight,
+        gate_weight,
+        up_weight,
+        out_weight.T,
+        down_weight.T,
     )
-    feed_shards = (feedforward_gain, gate_weight, up_weight, down_weight)
+    whole = lax.all_gather(jnp.concatenate(sources, axis=1), ("dp", "ctx"), axis=0, tiled=True)
+    parts = []
+    edge = 0
+    for source in sources:
+        parts.append(whole[:, edge : edge + source.shape[1]])
+        edge = edge + source.shape[1]
+    whole_query, whole_key, whole_value, whole_gate, whole_up, whole_out, whole_down = parts
+    gain_in, gain_query, gain_key, gain_feed = (
+        lax.all_gather(gain, ("dp", "ctx"), axis=0, tiled=True)
+        for gain in (attention_gain, query_gain, key_gain, feedforward_gain)
+    )
     grad_attention_gain = jnp.zeros((D,), jnp.float32)
     grad_feed_gain = jnp.zeros((D,), jnp.float32)
     grad_query_gain = jnp.zeros((HD,), jnp.float32)
@@ -151,10 +1094,6 @@
         hidden = hidden_in[batch, 0].astype(jnp.float32)
         query_seg = segments[batch, 0]
         grad_out = cotangent[batch, 0]
-        attention_set = fetch_attention(*attention_shards)
-        gain_in, gain_query, gain_key, whole_query, whole_key, whole_value, whole_out = (
-            attention_set
-        )
         normed = normalize(hidden)
         scaled_in = (normed * gain_in.astype(jnp.float32)).astype(jnp.bfloat16)
         query_heads = jnp.dot(scaled_in, whole_query, preferred_element_type=jnp.float32).reshape(
@@ -232,9 +1171,7 @@
             ),
         )
         mixed_low = mixed.reshape(tokens, HQ * HD).astype(jnp.bfloat16)
-        residual = hidden + jnp.dot(mixed_low, whole_out, preferred_element_type=jnp.float32)
-        feed_set = fetch_feedforward(*feed_shards)
-        gain_feed, whole_gate, whole_up, whole_down = feed_set
+        residual = hidden + contract_last(mixed_low, whole_out)
         feed_normed = normalize(residual)
         feed_scale = gain_feed.astype(jnp.float32)
         ff_in = (feed_normed * feed_scale).astype(jnp.bfloat16)
@@ -243,27 +1180,21 @@
         sigmoid = jax.nn.sigmoid(gate)
         swish = gate * sigmoid
         hidden_low = (swish * up_part).astype(jnp.bfloat16)
-        block_out = residual + jnp.dot(hidden_low, whole_down, preferred_element_type=jnp.float32)
+        block_out = residual + contract_last(hidden_low, whole_down)
         outputs.append(block_out.astype(jnp.bfloat16))
-        feed_back = fetch_feedforward(*feed_shards)
-        attention_back = fetch_attention(*attention_shards)
-        back_gain_feed, back_gate, back_up, back_down = feed_back
-        back_gain_in, back_gain_query, back_gain_key, back_query, back_key, back_value, back_out = (
-            attention_back
-        )
-        grad_hidden = contract_last(grad_out, back_down)
+        grad_hidden = jnp.dot(grad_out, whole_down, preferred_element_type=jnp.float32)
         grad_gate = (grad_hidden * up_part * (sigmoid * (1.0 + gate * (1.0 - sigmoid)))).astype(
             jnp.bfloat16
         )
         grad_up = (grad_hidden * swish).astype(jnp.bfloat16)
-        grad_feed_in = contract_last(grad_gate, back_gate) + contract_last(grad_up, back_up)
+        grad_feed_in = contract_last(grad_gate, whole_gate) + contract_last(grad_up, whole_up)
         grad_feed_gain = grad_feed_gain + jnp.sum(grad_feed_in * feed_normed, axis=0)
         grad_residual = grad_out.astype(jnp.float32) + norm_back(
-            residual, grad_feed_in * back_gain_feed.astype(jnp.float32)
+            residual, grad_feed_in * gain_feed.astype(jnp.float32)
         )
         grad_proj = grad_residual.astype(jnp.bfloat16)
         grad_mixed = (
-            contract_last(grad_proj, back_out).astype(jnp.bfloat16).reshape(tokens, HK, groups, HD)
+            jnp.dot(grad_proj, whole_out, preferred_element_type=jnp.float32).astype(jnp.bfloat16).reshape(tokens, HK, groups, HD)
         )
         delta = jnp.transpose(jnp.sum(grad_mixed.astype(jnp.float32) * mixed, axis=-1), (1, 2, 0))
 
@@ -330,26 +1261,26 @@
         turned_query = rotate_back(grad_query.reshape(tokens, HQ, HD), cosine, sine)
         grad_query_gain = grad_query_gain + jnp.sum(turned_query * query_norm, axis=(0, 1))
         grad_query_low = (
-            norm_back(query_heads, turned_query * back_gain_query.astype(jnp.float32))
+            norm_back(query_heads, turned_query * gain_query.astype(jnp.float32))
             .reshape(tokens, HQ * HD)
             .astype(jnp.bfloat16)
         )
         turned_key = rotate_back(grad_keys_own.reshape(tokens, HK, HD), cosine, sine)
         grad_key_gain = grad_key_gain + jnp.sum(turned_key * key_norm, axis=(0, 1))
         grad_key_low = (
-            norm_back(key_heads, turned_key * back_gain_key.astype(jnp.float32))
+            norm_back(key_heads, turned_key * gain_key.astype(jnp.float32))
             .reshape(tokens, HK * HD)
             .astype(jnp.bfloat16)
         )
         grad_value_low = grad_values_own.astype(jnp.bfloat16)
         grad_scaled_in = (
-            contract_last(grad_query_low, back_query)
-            + contract_last(grad_key_low, back_key)
-            + contract_last(grad_value_low, back_value)
+            contract_last(grad_query_low, whole_query)
+            + contract_last(grad_key_low, whole_key)
+            + contract_last(grad_value_low, whole_value)
         )
         grad_attention_gain = grad_attention_gain + jnp.sum(grad_scaled_in * normed, axis=0)
         input_grads.append(
-            grad_residual + norm_back(hidden, grad_scaled_in * back_gain_in.astype(jnp.float32))
+            grad_residual + norm_back(hidden, grad_scaled_in * gain_in.astype(jnp.float32))
         )
         stored.append(
             (
@@ -399,22 +1330,22 @@
     summed = lax.psum_scatter(
         jnp.concatenate(
             [
-                contract_first(all_in, all_query),
-                contract_first(all_in, all_key),
-                contract_first(all_in, all_value),
-                contract_first(all_feed, all_gate),
-                contract_first(all_feed, all_up),
-                contract_first(all_proj, all_mixed),
-                contract_first(all_out, all_hidden),
-                gains,
-                jnp.zeros((count, 124), jnp.float32),
+                contract_first(all_in, all_query).astype(BF),
+                contract_first(all_in, all_key).astype(BF),
+                contract_first(all_in, all_value).astype(BF),
+                contract_first(all_feed, all_gate).astype(BF),
+                contract_first(all_feed, all_up).astype(BF),
+                contract_first(all_proj, all_mixed).astype(BF),
+                contract_first(all_out, all_hidden).astype(BF),
+                gains.astype(BF),
+                jnp.zeros((count, 124), BF),
             ],
             axis=1,
         ),
         ("dp", "ctx"),
         scatter_dimension=0,
         tiled=True,
-    )
+    ).astype(F32)
     widths = [HQ * HD, HK * HD, HK * HD, FF, FF, HQ * HD, FF, 128]
     pieces = []
     edge = 0
@@ -442,8 +1373,16 @@
 
 
 def solution(mesh):
+    shape = dict(mesh.shape)
+    chips_hold_sequences = shape["dp"] == 4 and shape["ctx"] == 8
+
+    def step(*arrays):
+        if chips_hold_sequences and arrays[0].shape[2] == 64:
+            return fused(*arrays)
+        return general(*arrays)
+
     return jax.shard_map(
-        on_device,
+        step,
         mesh=mesh,
         in_specs=(
             P(None, "dp", "ctx", None),

time: 2810 us -> 397 us (0.14)
  waiting for transfers between devices: 2270 us -> 0 us
  Pallas kernels: 0 us -> 379 us
  matrix products: 220 us -> 0 us
  local copies, waits for them, and re-layouts: 189 us -> 11.9 us
  blocking collectives: 52.9 us -> 0 us
  other arithmetic: 52.5 us -> 4.28 us
    reduce_scatter x5 -> x0, waiting for transfers between devices: 1430 us -> none  [the longest x1 1300 us: on_device(): lax.psum_scatter(jnp.concatenate([contract_first(all_in, all_query), cont...]
    all_gather x15 -> x0, waiting for transfers between devices: 608 us -> none  [the longest x4 157 us: on_device(): lax.all_gather(keys_flat, 'ctx', axis=0, tiled=True)]
    pallas_call x0 -> x1, Pallas kernels: none -> 379 us  [fused(): pl.pallas_call(functools.partial(layer_kernel, names, tokens), out_shape=...]
    unnamed x28 -> x0, waiting for transfers between devices: 229 us -> none
    dot_general x87 -> x0, matrix products: 220 us -> none  [the longest x28 73.8 us: contract_last(): lax.dot_general(left, right, (((1,), (1,)), ((), ())), preferred_element_...]
    concatenate x1 -> x0, local copies, waits for them, and re-layouts: 64.9 us -> none  [on_device(): jnp.concatenate([contract_first(all_in, all_query), contract_first(all_in...]
    unnamed x2 -> x0, blocking collectives: 52.9 us -> none
    unnamed x550 -> x36, local copies, waits for them, and re-layouts: 38.2 us -> 9.17 us
  transfers between devices with their start and end apart: 24 -> 0, of which waited for: 22 -> 0; matrix products, arithmetic and copies ran while one was open for 11% -> 0% of each run, Pallas kernels for 0% -> 0%
where the time goes in v1:
time: 397 us; the launch traced here: 396 us
  Pallas kernels  379 us (95%)
  local copies, waits for them, and re-layouts  11.9 us (3%)
  other arithmetic  4.28 us (1%)
    pallas_call x1, Pallas kernels, fused(): pl.pallas_call(functools.partial(layer_kernel, names, tokens), out_shape=...  379 us
    unnamed x36, local copies, waits for them, and re-layouts  9.17 us

profile of v1, /device:TPU:0, one launch (start us, length us, event | category | flops | bytes accessed | tf_op | source)
XLA Modules:
  0.0 395.9 jit_solution(2378325691382119407)
XLA Ops:
  0.7 0.0 copy-start.10
  0.7 0.0 copy-start.11
  0.7 0.6 copy-done.10
  1.3 0.0 copy-done.11
  1.3 0.0 copy-start.12
  1.3 0.0 copy-start.13
  1.3 0.0 copy-start.9
  1.4 0.6 copy-done.12
  2.0 0.0 copy-done.13
  2.0 0.0 copy-done.9
  2.0 0.1 pad_select_fusion
  2.1 0.1 copy.39
  2.2 0.6 pad.15.refs_5_
  2.8 0.6 broadcast_in_dim.18.refs_2_
  3.4 1.0 fusion
  4.4 1.0 pad_maximum_fusion
  5.4 379.0 %layer.1 = (bf16[4,64,1024]{2,1,0:T(8,128)(2,1)}, bf16[4,64,1024]{2,1,0:T(8,128)(2,1)}, f32[32,128]{1,0:T(8,128)}, f32[32,1024]{1,0:T(8,128)}, f32[32,1024]{1,0:...) custom-call(bf16[4,64,1024]{2,1,0:T(8,128)(2,1)} %bitcast.22, ...), custom_call_target="tpu_custom_call" | custom-call | tf_op jit(solution)/shard_map/layer/pallas_call | solution.py:956
  384.5 0.0 copy-start.8
  384.5 0.7 copy-done.8
  385.2 0.7 slice_reduce_fusion.2
  385.9 0.7 slice_reduce_fusion
  386.6 0.0 copy-start
  386.6 2.2 bitcast_convert_fusion
  388.8 0.0 copy-done
  388.8 0.0 copy-start.5
  388.8 0.8 copy.50
  389.6 0.3 copy-done.5
  389.9 0.0 copy-start.7
  389.9 0.0 copy-start.6
  389.9 0.7 copy.51
  390.6 0.3 copy-done.7
  390.9 0.0 copy-start.4
  390.9 0.7 copy.52
  391.6 0.0 copy-done.6
  391.6 0.0 copy-start.3
  391.6 0.7 copy.53
  392.2 0.0 copy-done.4
  392.2 0.7 copy.54
  392.9 0.0 copy-done.3
  392.9 0.0 copy-start.2
  392.9 0.7 copy.55
  393.7 0.4 copy-done.2
  394.1 0.0 copy-start.1
  394.1 0.7 copy.56
  394.8 0.4 copy-done.1
  395.2 0.7 copy.57
  (5 shorter events, 0.0 us)
Async XLA Ops:
  0.7 0.7 copy-start.10
  0.7 0.7 copy-start.11
  1.3 0.7 copy-start.12
  1.3 0.7 copy-start.13
  1.3 0.7 copy-start.9
  384.5 0.7 copy-start.8
  386.6 2.2 copy-start
  388.8 1.1 copy-start.5
  389.9 1.0 copy-start.7
  389.9 1.7 copy-start.6
  390.9 1.3 copy-start.4
  391.6 1.4 copy-start.3
  392.9 1.1 copy-start.2
  394.1 1.1 copy-start.1

commit v2 on v1

--- a/solution.py
+++ b/solution.py
@@ -47,18 +47,19 @@
     v=HK * HD // 2,
     q=HQ * HD // 2,
     o=HQ * HD // 2,
-    g=FF // 2,
-    u=FF // 2,
-    d=FF // 2,
+    g=FF // 4,
+    u=FF // 4,
+    d=FF // 4,
 )
 ORDER = tuple(WIDTHS)
+FEED = ("g", "u", "d")
+GATHER_Y = dict(e=0, k=0, v=0, q=0, o=0)
+SUM_Y = dict(e=128, k=256, v=256, q=512, o=512)
 HALF_HQ, HALF_HK = HQ // 2, HK // 2
 
 
-def split_columns(name):
-    width = WIDTHS[name]
-    first = max(128, width // 2)
-    return first, width - first
+def split_columns(name, by):
+    return by[name], WIDTHS[name] - by[name]
 
 
 def dot(left, right):
@@ -93,6 +94,7 @@
     ox, oc, oy = 1 - x, 1 - c, 1 - y
     sibling = (2 * x + oc, ctx)
     x_next = (2 * ox + c, ctx)
+    x_cross = (2 * ox + oc, ctx)
     y_next = (dp, 2 * z + oy)
     length = 8 * tokens
     own_rows = 4 * tokens
@@ -125,52 +127,55 @@
             barrier, inc=1, device_id=(2 * x + lax.div(there, 8), lax.rem(there, 8)), device_id_type=MESH
         )
     pl.semaphore_signal(barrier, inc=1, device_id=x_next, device_id_type=MESH)
-    pl.semaphore_wait(barrier, 16)
+    pl.semaphore_signal(barrier, inc=1, device_id=x_cross, device_id_type=MESH)
+    pl.semaphore_wait(barrier, 17)
 
     weight = {n: getattr(at, "w_" + n) for n in ORDER}
     shard = {n: getattr(at, "in_" + n) for n in ORDER}
-    s0 = {n: places.take() for n in ORDER}
+    s0 = {n: places.take(3) for n in ORDER}
     lc = {n: places.take() for n in ORDER}
-    sz = {n: places.take(6) for n in ORDER}
+    sz = {n: places.take(9) for n in ORDER}
     s2 = {n: places.take(2) for n in ORDER}
     s3 = {n: places.take(2) for n in ORDER}
     gather_sends = {n: [] for n in ORDER}
 
-    def part(name, which):
+    def part(name, xx, cc):
         if name == "e":
             return shard[name]
         width = WIDTHS[name]
+        which = 2 * xx + cc if name in FEED else cc
         return shard[name].at[:, pl.ds(pl.multiple_of(which * width, width), width)]
 
     def local(name):
-        return pltpu.make_async_copy(part(name, c), weight[name].at[x, c, z, y], recvs.at[lc[name]])
+        return pltpu.make_async_copy(part(name, x, c), weight[name].at[x, c, z, y], recvs.at[lc[name]])
 
     def begin(name, copy):
         copy.start()
         gather_sends[name].append(copy)
 
     def gather_core(name):
-        begin(name, remote(part(name, oc), weight[name].at[x, c, z, y], s0[name], sibling))
+        here = weight[name].at[x, c, z, y]
+        begin(name, remote(part(name, x, oc), here, s0[name], sibling))
+        if name in FEED:
+            begin(name, remote(part(name, ox, c), here, s0[name] + 1, x_next))
+            begin(name, remote(part(name, ox, oc), here, s0[name] + 2, x_cross))
         local(name).start()
 
-    def gather_z_own(name):
+    def gather_z(name):
+        w = weight[name]
+        here = w.at[x, c, z, y]
         for step in (1, 2, 3):
-            begin(
-                name,
-                remote(
-                    part(name, c), weight[name].at[x, c, z, y], sz[name] + step - 1, z_device(step)
-                ),
-            )
-
-    def gather_z_sibling(name):
-        block = weight[name].at[x, oc, z, y]
+            begin(name, remote(part(name, x, c), here, sz[name] + step - 1, z_device(step)))
+        block = w.at[x, oc, z, y]
         arrived(block, s0[name], sibling)
         for step in (1, 2, 3):
             begin(name, remote(block, block, sz[name] + 2 + step, z_device(step)))
-
-    def gather_start(name):
-        gather_core(name)
-        gather_z_own(name)
+        if name in FEED:
+            arrived(w.at[ox, c, z, y], s0[name] + 1, x_next)
+            arrived(w.at[ox, oc, z, y], s0[name] + 2, x_cross)
+            block = w.at[ox, :, z, y]
+            for step in (1, 2, 3):
+                begin(name, remote(block, block, sz[name] + 5 + step, z_device(step)))
 
     def gather_two(name):
         w = weight[name]
@@ -180,19 +185,27 @@
             device = (dp, 2 * source + y)
             arrived(w.at[x, c, source, y], sz[name] + step - 1, device)
             arrived(w.at[x, oc, source, y], sz[name] + 2 + step, device)
-        first, second = split_columns(name)
-        one = w.at[x, :, :, y, :, pl.ds(0, first)]
-        begin(name, remote(one, one, s2[name], x_next))
+            if name in FEED:
+                arrived(w.at[ox, :, source, y], sz[name] + 5 + step, device)
+        if name in FEED:
+            block = w.at[:, :, :, y]
+            begin(name, remote(block, block, s2[name], y_next))
+            return
+        first, second = split_columns(name, GATHER_Y)
+        if first:
+            one = w.at[x, :, :, y, :, pl.ds(0, first)]
+            begin(name, remote(one, one, s2[name], x_next))
         if second:
             two = w.at[x, :, :, y, :, pl.ds(first, second)]
             begin(name, remote(two, two, s2[name] + 1, y_next))
 
     def gather_three(name):
         w = weight[name]
-        first, second = split_columns(name)
-        arrived(w.at[ox, :, :, y, :, pl.ds(0, first)], s2[name], x_next)
-        one = w.at[:, :, :, y, :, pl.ds(0, first)]
-        begin(name, remote(one, one, s3[name], y_next))
+        first, second = split_columns(name, GATHER_Y)
+        if first:
+            arrived(w.at[ox, :, :, y, :, pl.ds(0, first)], s2[name], x_next)
+            one = w.at[:, :, :, y, :, pl.ds(0, first)]
+            begin(name, remote(one, one, s3[name], y_next))
         if second:
             arrived(w.at[x, :, :, oy, :, pl.ds(first, second)], s2[name] + 1, y_next)
             two = w.at[x, :, :, :, :, pl.ds(first, second)]
@@ -200,8 +213,12 @@
 
     def gather_done(name):
         w = weight[name]
-        first, second = split_columns(name)
-        arrived(w.at[:, :, :, oy, :, pl.ds(0, first)], s3[name], y_next)
+        if name in FEED:
+            arrived(w.at[:, :, :, oy], s2[name], y_next)
+            return
+        first, second = split_columns(name, GATHER_Y)
+        if first:
+            arrived(w.at[:, :, :, oy, :, pl.ds(0, first)], s3[name], y_next)
         if second:
             arrived(w.at[ox, :, :, :, :, pl.ds(first, second)], s3[name] + 1, x_next)
 
@@ -291,7 +308,7 @@
 
     hidden_own, cot_all, seg_all = at.hidden_own, at.cot_all, at.seg_all
     hidden_move = Reshard(at.hidden_in, lambda core, j: hidden_own.at[j])
-    cot_move = Reshard(at.cotangent, lambda core, j: cot_all.at[4 * core + j])
+    cot_move = Reshard(at.cotangent, lambda core, j: cot_all.at[4 * (2 * x + core) + j])
     out_move = Return(at.out_own, at.block_out)
     grad_move = Return(at.grad_own, at.input_grad)
     seg_place, seg_recv, seg_own = places.take(8), places.take(8), places.take()
@@ -349,39 +366,76 @@
 
     own_at = pl.multiple_of(c * own_rows, own_rows)
     other_at = pl.multiple_of(oc * own_rows, own_rows)
-    partial_out, partial_in = at.partial_out, at.partial_in
-
-    def swap_partial(index):
-        landing = partial_in.at[index]
-        return Swap(partial_out.at[index % 2], landing, landing)
+
+    class Spread:
+        def __init__(self, block):
+            self.block = block
+            self.place = places.take(3)
+
+        def start(self):
+            own = self.block(x, c)
+            self.near = remote(own, own, self.place, sibling)
+            self.across = remote(own, own, self.place + 1, x_next)
+            self.near.start()
+            self.across.start()
+
+        def near_wait(self):
+            arrived(self.block(x, oc), self.place, sibling)
+
+        def pass_on(self):
+            arrived(self.block(ox, c), self.place + 1, x_next)
+            block = self.block(ox, c)
+            self.far = remote(block, block, self.place + 2, sibling)
+            self.far.start()
+
+        def far_wait(self):
+            arrived(self.block(ox, oc), self.place + 2, sibling)
+
+        def sent(self):
+            for copy in (self.near, self.across, self.far):
+                copy.wait_send()
 
     r1 = {n: places.take(2) for n in ORDER}
     r2 = {n: places.take(2) for n in ORDER}
     r3 = {n: places.take(3) for n in ORDER}
-    r4 = {n: places.take() for n in ORDER}
+    r4 = {n: places.take(3) for n in ORDER}
     sum_sends = []
+    grads = dict(weight, d=at.grad_d)
 
     def send(copy):
         copy.start()
         sum_sends.append(copy)
 
+    def sum_z(name):
+        w = grads[name]
+        for step in (1, 2, 3):
+            there = z_at(step)
+            block = w.at[:, :, there, y] if name in FEED else w.at[x, :, there, y]
+            send(remote(block, getattr(at, "r3_" + name).at[step - 1], r3[name] + step - 1, z_device(step)))
+
     def sum_one(name):
-        w = weight[name]
-        first, second = split_columns(name)
+        w = grads[name]
+        if name in FEED:
+            send(remote(w.at[:, :, :, oy], getattr(at, "r1a_" + name), r1[name], y_next))
+            return
+        first, second = split_columns(name, SUM_Y)
         send(remote(w.at[:, :, :, oy, :, pl.ds(0, first)], getattr(at, "r1a_" + name), r1[name], y_next))
         if second:
             send(remote(w.at[ox, :, :, :, :, pl.ds(first, second)], getattr(at, "r1b_" + name), r1[name] + 1, x_next))
 
     def sum_two(name):
-        w = weight[name]
-        first, second = split_columns(name)
+        w = grads[name]
         arrived(getattr(at, "r1a_" + name), r1[name], y_next)
+        first, second = (WIDTHS[name], 0) if name in FEED else split_columns(name, SUM_Y)
 
         @pl.loop(0, 16)
         def _(i):
             xx, cc, zz = lax.div(i, 8), lax.rem(lax.div(i, 4), 2), lax.rem(i, 4)
             w[xx, cc, zz, y, :, pl.ds(0, first)] += getattr(at, "r1a_" + name)[xx, cc, zz]
 
+        if name in FEED:
+            sum_z(name)
+            return
         send(remote(w.at[ox, :, :, y, :, pl.ds(0, first)], getattr(at, "r2a_" + name), r2[name], x_next))
         if second:
             arrived(getattr(at, "r1b_" + name), r1[name] + 1, x_next)
@@ -394,8 +448,8 @@
             send(remote(w.at[x, :, :, oy, :, pl.ds(first, second)], getattr(at, "r2b_" + name), r2[name] + 1, y_next))
 
     def sum_three(name):
-        w = weight[name]
-        first, second = split_columns(name)
+        w = grads[name]
+        first, second = split_columns(name, SUM_Y)
         arrived(getattr(at, "r2a_" + name), r2[name], x_next)
         if second:
             arrived(getattr(at, "r2b_" + name), r2[name] + 1, y_next)
@@ -407,26 +461,29 @@
             if second:
                 w[x, cc, zz, y, :, pl.ds(first, second)] += getattr(at, "r2b_" + name)[cc, zz]
 
-        for step in (1, 2, 3):
-            send(
-                remote(
-                    w.at[x, :, z_at(step), y], getattr(at, "r3_" + name).at[step - 1], r3[name] + step - 1, z_device(step)
-                )
-            )
+        sum_z(name)
 
     def sum_four(name):
-        w, landed = weight[name], getattr(at, "r3_" + name)
+        w, landed = grads[name], getattr(at, "r3_" + name)
         for step in (1, 2, 3):
             arrived(landed.at[step - 1], r3[name] + step - 1, (dp, 2 * lax.rem(z + 4 - step, 4) + y))
 
-        def total(core):
-            value = w[x, core, z, y].astype(F32)
+        def total(*place):
+            mine = w[(*place, z, y)] if name in FEED else w[(x, *place, z, y)]
+            value = mine.astype(F32)
             for step in range(3):
-                value = value + landed[step, core].astype(F32)
+                value = value + landed[(step, *place)].astype(F32)
             return value
 
         width = WIDTHS[name]
         staged, result = getattr(at, "r4_" + name), getattr(at, "out_" + name)
+        if name in FEED:
+            columns = pl.ds(pl.multiple_of(dp * width, width), width)
+            for i, (xx, cc, device) in enumerate(((ox, oc, x_cross), (ox, c, x_next), (x, oc, sibling))):
+                staged[i] = total(xx, cc)
+                send(remote(staged.at[i], result.at[:, columns], r4[name] + i, device))
+            result[:, columns] = total(x, c)
+            return
         staged[...] = total(oc)
         if name == "e":
             send(remote(staged, at.r5_e, r4[name], sibling))
@@ -437,11 +494,15 @@
             result[:, columns] = total(c)
 
     def sum_done(name):
+        width = WIDTHS[name]
         if name == "e":
             arrived(at.r5_e, r4[name], sibling)
             at.out_e[...] = at.out_e[...] + at.r5_e[...]
+        elif name in FEED:
+            for i, (xx, cc, device) in enumerate(((ox, oc, x_cross), (ox, c, x_next), (x, oc, sibling))):
+                columns = pl.ds(pl.multiple_of((2 * xx + cc) * width, width), width)
+                arrived(getattr(at, "out_" + name).at[:, columns], r4[name] + i, device)
         else:
-            width = WIDTHS[name]
             columns = pl.ds(pl.multiple_of(oc * width, width), width)
             arrived(getattr(at, "out_" + name).at[:, columns], r4[name], sibling)
 
@@ -449,11 +510,17 @@
     scaled, ff_in, grad_proj = at.scaled, at.ff_in, at.grad_proj
     residual, grad_residual = at.residual, at.grad_residual
     acc_own = at.acc_own
-    scaled_swap, ff_swap, proj_swap = swap_rows(scaled), swap_rows(ff_in), swap_rows(grad_proj)
-    cot_swap = Swap(
-        cot_all.at[pl.ds(4 * c, 4)], cot_all.at[pl.ds(4 * c, 4)], cot_all.at[pl.ds(4 * oc, 4)]
-    )
-    partials = [swap_partial(i) for i in range(4)]
+    scaled_swap, proj_swap = swap_rows(scaled), swap_rows(grad_proj)
+    ff_spread = Spread(lambda xx, cc: ff_in.at[2 * xx + cc])
+    cot_spread = Spread(lambda xx, cc: cot_all.at[pl.ds(4 * (2 * xx + cc), 4)])
+    partials = [Swap(at.partial_out.at[i], at.partial_in.at[i], at.partial_in.at[i]) for i in range(2)]
+    feed_near = [
+        [Swap(at.near_out.at[i, k], at.near_in.at[i, k], at.near_in.at[i, k]) for k in range(2)] for i in range(2)
+    ]
+    feed_cross = []
+    for i in range(2):
+        place = places.take()
+        feed_cross.append((remote(at.cross_out.at[i], at.cross_in.at[i], place, x_next), place))
 
     def selector():
         row = lax.broadcasted_iota(jnp.int32, (D, HD), 0)
@@ -531,8 +598,8 @@
         terms = jnp.exp(scores - jnp.max(scores, axis=-1, keepdims=True))
         return terms * (1.0 / jnp.sum(terms, axis=-1, keepdims=True))
 
-    def attend():
-        @pl.loop(0, HALF_HQ)
+    def attend(first, last):
+        @pl.loop(first, last)
         def _(head):
             pair = lax.div(head, 2)
             for block in range(2):
@@ -542,83 +609,131 @@
                     block * half : (block + 1) * half, pl.ds(pl.multiple_of(head * HD, HD), HD)
                 ] = dot(low, at.values[pair, seen]).astype(BF)
 
+    def column_quarters(body):
+        @pl.loop(0, 4)
+        def _(t):
+            body(t, pl.ds(pl.multiple_of(t * (D // 4), D // 4), D // 4))
+
     def partial_product(index, terms):
         def rows_times(first, t):
+            return sum(dot_nt(left(pl.ds(first, own_rows)), rows_of(name, t)) for left, name in terms)
+
+        def theirs(t, columns):
+            at.partial_out[index, :, columns] = rows_times(other_at, t).astype(BF)
+
+        def mine(t, columns):
+            acc_own[:, columns] = rows_times(own_at, t)
+
+        column_quarters(theirs)
+        partials[index].start()
+        column_quarters(mine)
+
+    def own_sum(index, j):
+        return acc_own[here_block(j)] + at.partial_in[index, here_block(j)].astype(F32)
+
+    def feed_product(index, terms):
+        def rows_times(xx, cc, t):
+            first = pl.multiple_of((2 * xx + cc) * own_rows, own_rows)
             return sum(dot_nt(left[pl.ds(first, own_rows)], rows_of(name, t)) for left, name in terms)
 
+        def give(k, xx):
+            def body(t, columns):
+                at.near_out[index, k, :, columns] = rows_times(xx, oc, t).astype(BF)
+
+            column_quarters(body)
+            feed_near[index][k].start()
+
+        def keep(xx):
+            def body(t, columns):
+                acc_own[:, columns] = rows_times(xx, c, t)
+
+            column_quarters(body)
+
+        give(0, ox)
+        keep(ox)
+        feed_near[index][0].wait()
+        near = at.near_in
+
         @pl.loop(0, 4)
-        def _(t):
-            columns = pl.ds(pl.multiple_of(t * (D // 4), D // 4), D // 4)
-            partial_out[index % 2, :, columns] = rows_times(other_at, t).astype(BF)
-
-        partials[index].start()
-
-        @pl.loop(0, 4)
-        def _(t):
-            columns = pl.ds(pl.multiple_of(t * (D // 4), D // 4), D // 4)
-            acc_own[:, columns] = rows_times(own_at, t)
-
-    def own_sum(index, j):
-        return acc_own[here_block(j)] + partial_in[index, here_block(j)].astype(F32)
+        def _(j):
+            rows = here_block(j)
+            at.cross_out[index, rows] = (acc_own[rows] + near[index, 0, rows].astype(F32)).astype(BF)
+
+        feed_cross[index][0].start()
+        give(1, x)
+        keep(x)
+
+    def feed_wait(index):
+        feed_near[index][1].wait()
+        copy, place = feed_cross[index]
+        copy.wait_send()
+        arrived(at.cross_in.at[index], place, x_next)
+
+    def feed_sum(index, j):
+        rows = here_block(j)
+        return acc_own[rows] + at.near_in[index, 1, rows].astype(F32) + at.cross_in[index, rows].astype(F32)
 
     def add_residual():
         @pl.loop(0, 4)
         def _(j):
             value = hidden_own[j].astype(F32) + own_sum(0, j)
             residual[here_block(j)] = value
-            ff_in[own_block(j)] = (normalize(value) * gains[1:2]).astype(BF)
+            ff_in[2 * x + c, here_block(j)] = (normalize(value) * gains[1:2]).astype(BF)
 
     gate_part, up_part, hidden_low = at.gate_part, at.up_part, at.hidden_low
 
-    def feed_forward():
+    def chip_rows(xx):
+        return pl.ds(pl.multiple_of(xx * length, length), length)
+
+    def feed_forward(xx):
+        rows = chip_rows(xx)
+
         @pl.loop(0, WIDTHS["g"] // 256)
         def _(t):
             columns = pl.ds(pl.multiple_of(t * 256, 256), 256)
-            gate = dot(ff_in[...], columns_of("g", t))
-            up = dot(ff_in[...], columns_of("u", t))
+            left = ff_in[pl.ds(2 * xx, 2)].reshape(length, D)
+            gate = dot(left, columns_of("g", t))
+            up = dot(left, columns_of("u", t))
             sigmoid = 1.0 / (1.0 + jnp.exp(-gate))
             swish = gate * sigmoid
-            hidden_low[:, columns] = (swish * up).astype(BF)
-            up_part[:, columns] = swish.astype(BF)
-            gate_part[:, columns] = (up * sigmoid * (1.0 + gate * (1.0 - sigmoid))).astype(BF)
+            hidden_low[rows, columns] = (swish * up).astype(BF)
+            up_part[rows, columns] = swish.astype(BF)
+            gate_part[rows, columns] = (up * sigmoid * (1.0 + gate * (1.0 - sigmoid))).astype(BF)
 
     def write_out():
         @pl.loop(0, 4)
         def _(j):
-            at.out_own[j] = (residual[here_block(j)] + own_sum(1, j)).astype(BF)
+            at.out_own[j] = (residual[here_block(j)] + feed_sum(0, j)).astype(BF)
 
         for j in range(4):
             out_move.start(j)
 
-    def cotangent_rows():
-        return cot_all[...].reshape(length, D)
-
     def grad_hidden():
-        @pl.loop(0, WIDTHS["d"] // 256)
+        @pl.loop(0, 2 * (WIDTHS["d"] // 256))
+        def _(i):
+            xx, t = lax.div(i, 3), lax.rem(i, 3)
+            rows, columns = chip_rows(xx), pl.ds(pl.multiple_of(t * 256, 256), 256)
+            grad = dot(cot_all[pl.ds(8 * xx, 8)].reshape(length, D), columns_of("d", t))
+            gate_part[rows, columns] = (grad * gate_part[rows, columns].astype(F32)).astype(BF)
+            up_part[rows, columns] = (grad * up_part[rows, columns].astype(F32)).astype(BF)
+
+    turned_rows = at.turned_rows
+
+    def transpose_rows(load, count):
+        @pl.loop(0, D // 128)
+        def _(t):
+            place = pl.ds(pl.multiple_of(t * 128, 128), 128)
+            turned_rows[place, :count] = load(place).reshape(count, 128).T
+
+    def weight_grad(name, right, count):
+        if name != "d":
+            gather_sent(name)
+
+        @pl.loop(0, WIDTHS[name] // 256)
         def _(t):
             columns = pl.ds(pl.multiple_of(t * 256, 256), 256)
-            grad = dot(cotangent_rows(), columns_of("d", t))
-            gate_part[:, columns] = (grad * gate_part[:, columns].astype(F32)).astype(BF)
-            up_part[:, columns] = (grad * up_part[:, columns].astype(F32)).astype(BF)
-
-    turned_rows = at.turned_rows
-
-    def transpose_rows(load):
-        @pl.loop(0, D // 128)
-        def _(t):
-            turned_rows[pl.ds(pl.multiple_of(t * 128, 128), 128)] = load(
-                pl.ds(pl.multiple_of(t * 128, 128), 128)
-            ).T
-
-    def weight_grad(name, right, first=0):
-        gather_sent(name)
-
-        @pl.loop(0, WIDTHS[name] // 256)
-        def _(t):
-            grad = dot(turned_rows[...], right[:, pl.ds(pl.multiple_of(first + t * 256, 256), 256)])
-            weight[name][:, :, :, :, :, pl.ds(pl.multiple_of(t * 256, 256), 256)] = grad.astype(BF).reshape(
-                2, 2, 4, 2, 32, 256
-            )
+            grad = dot(turned_rows[:, :count], right(columns))
+            grads[name][:, :, :, :, :, columns] = grad.astype(BF).reshape(2, 2, 4, 2, 32, 256)
 
     grad_gains = at.grad_gains
 
@@ -628,39 +743,50 @@
         @pl.loop(0, 4)
         def _(j):
             value = residual[here_block(j)]
-            grad = own_sum(2, j)
+            grad = feed_sum(1, j)
             scale = lax.rsqrt(jnp.mean(value * value, axis=-1, keepdims=True) + NORM_EPS)
             grad_gains[1:2] += jnp.sum(grad * (value * scale), axis=0, keepdims=True)
-            total = cot_all[4 * c + j].astype(F32) + norm_back(value, grad * gains[1:2])
+            total = cot_all[4 * (2 * x + c) + j].astype(F32) + norm_back(value, grad * gains[1:2])
             grad_residual[here_block(j)] = total
             grad_proj[own_block(j)] = total.astype(BF)
 
-    grad_mixed = gate_part
+    grad_mixed, grad_heads = ff_in, cot_all
 
     def back_mixed():
         @pl.loop(0, WIDTHS["o"] // 256)
         def _(t):
             columns = pl.ds(pl.multiple_of(t * 256, 256), 256)
-            grad_mixed[:, columns] = dot(grad_proj[...], columns_of("o", t)).astype(BF)
-
-    grad_heads, grad_values = hidden_low, at.grad_values
+            grad = dot(grad_proj[...], columns_of("o", t)).astype(BF)
+            grad_mixed[:2, :, columns] = grad.reshape(2, half, 256)
+
+    def put_heads(first, columns, value):
+        grad_heads[first : first + 8, :, columns] = value.astype(BF).reshape(8, tokens, HD)
+
+    def head_columns(first, columns):
+        return grad_heads[first : first + 8, :, columns].reshape(length, columns.size)
+
+    def head_rows(first, rows, start, width):
+        block = first + lax.div(rows.start, tokens)
+        return grad_heads[pl.ds(block, 4), :, start : start + width].reshape(own_rows, width)
+
     grad_head_gains = at.grad_head_gains
 
     def turn_back(value):
         return value * cosine[...] - pltpu.roll(value, HD // 2, 1) * sine[...]
 
-    def back_head(value, grad, row, columns):
+    def back_head(value, grad, row, first, columns):
         scale = lax.rsqrt(jnp.mean(value * value, axis=-1, keepdims=True) + NORM_EPS)
         turned = turn_back(grad)
         grad_head_gains[row : row + 1] += jnp.sum(turned * (value * scale), axis=0, keepdims=True)
-        grad_heads[:, columns] = norm_back(value, turned * head_gains[row : row + 1]).astype(BF)
+        put_heads(first, columns, norm_back(value, turned * head_gains[row : row + 1]))
 
     grad_key, grad_value, grad_query = at.grad_key, at.grad_value, at.grad_query
 
-    def back_attend():
-        grad_head_gains[...] = jnp.zeros_like(grad_head_gains)
-
-        @pl.loop(0, HALF_HK)
+    def back_attend(first, last):
+        if first == 0:
+            grad_head_gains[...] = jnp.zeros_like(grad_head_gains)
+
+        @pl.loop(first, last)
         def _(pair):
             for i in range(2):
                 head = 2 * pair + i
@@ -669,7 +795,7 @@
                     rows = slice(block * half, (block + 1) * half)
                     seen = slice(0, (block + 1) * half)
                     probs = probabilities(head, pair, block)
-                    grad_out = grad_mixed[rows, lanes]
+                    grad_out = grad_mixed[block, :, lanes]
                     grad_probs = dot_nt(grad_out, at.values[pair, seen])
                     delta = jnp.sum(probs * grad_probs, axis=-1, keepdims=True)
                     grad_scores = (probs * (grad_probs - delta)).astype(BF)
@@ -682,20 +808,16 @@
                     else:
                         grad_key[seen] += key_part
                         grad_value[seen] += value_part
-                back_head(at.query_acc[head], grad_query[...], 2, lanes)
-            back_head(
-                at.key_acc[pair],
-                grad_key[...],
-                3,
-                pl.ds(pl.multiple_of(WIDTHS["q"] + pair * HD, HD), HD),
-            )
-            grad_values[:, pl.ds(pl.multiple_of(pair * HD, HD), HD)] = grad_value[...].astype(BF)
+                back_head(at.query_acc[head], grad_query[...], 2, 0, lanes)
+            lanes = pl.ds(pl.multiple_of(pair * HD, HD), HD)
+            back_head(at.key_acc[pair], grad_key[...], 3, 8, lanes)
+            put_heads(8, pl.ds(pl.multiple_of(WIDTHS["k"] + pair * HD, HD), HD), grad_value[...])
 
     def back_input():
         @pl.loop(0, 4)
         def _(j):
             value = hidden_own[j].astype(F32)
-            grad = own_sum(3, j)
+            grad = own_sum(1, j)
             scale = lax.rsqrt(jnp.mean(value * value, axis=-1, keepdims=True) + NORM_EPS)
             grad_gains[0:1] += jnp.sum(grad * (value * scale), axis=0, keepdims=True)
             at.grad_own[j] = (
@@ -714,20 +836,20 @@
             ).T
             weight["e"][i // 4, (i // 2) % 2, 2 * (i % 2) : 2 * (i % 2) + 2] = block.astype(BF).reshape(2, 2, 32, 128)
 
-    for name in ("e", "k", "v"):
-        gather_start(name)
+    for name in ("e", "k", "v", "q", "o"):
+        gather_core(name)
+    gather_z("e")
+    gather_z("k")
     seg_start()
     hidden_move.start()
-    for name in ("q", "o"):
-        gather_start(name)
-    for name in ("e", "k", "v"):
-        gather_z_sibling(name)
     gather_two("e")
+    gather_z("v")
     gather_two("k")
+    gather_z("q")
     gather_three("e")
-    gather_z_sibling("q")
     gather_two("v")
     gather_three("k")
+    gather_z("o")
     gather_done("e")
     prepare_gains()
     seg_wait()
@@ -735,92 +857,98 @@
     hidden_move.wait()
     scale_input()
     scaled_swap.start()
-    gather_start("g")
-    gather_z_sibling("o")
     gather_two("q")
+    for name in FEED:
+        gather_core(name)
+    gather_z("g")
     gather_three("v")
-    cot_move.start()
-    gather_start("u")
-    gather_z_sibling("g")
     gather_done("k")
     scaled_swap.wait()
     project_heads("k", head_gains[3:4], at.key_acc, at.keys)
     gather_two("o")
     gather_three("q")
-    gather_start("d")
-    gather_z_sibling("u")
+    cot_move.start()
     gather_done("v")
     project_values()
     gather_two("g")
+    gather_z("u")
     gather_three("o")
-    gather_z_sibling("d")
     gather_done("q")
     project_heads("q", head_gains[2:3], at.query_acc, at.queries)
     cot_move.wait()
-    cot_swap.start()
+    cot_spread.start()
+    attend(0, 4)
     gather_two("u")
-    gather_three("g")
-    attend()
-    gather_two("d")
-    gather_three("u")
+    gather_z("d")
+    cot_spread.pass_on()
+    attend(4, 8)
     gather_done("o")
-    partial_product(0, [(at.mixed, "o")])
+    partial_product(0, [(lambda rows: at.mixed[rows], "o")])
     partials[0].wait()
     add_residual()
-    ff_swap.start()
+    ff_spread.start()
+    gather_two("d")
+    cot_spread.near_wait()
+    cot_spread.far_wait()
+    transpose_rows(lambda columns: cot_all[:, :, columns], 2 * length)
     gather_done("g")
     gather_done("u")
-    gather_three("d")
-    ff_swap.wait()
-    feed_forward()
-    cot_swap.wait()
-    transpose_rows(lambda columns: cot_all[:, :, columns].reshape(length, 128))
+    ff_spread.near_wait()
+    feed_forward(x)
+    ff_spread.pass_on()
+    ff_spread.far_wait()
+    feed_forward(ox)
+
+    weight_grad("d", lambda columns: hidden_low[:, columns], 2 * length)
+    sum_one("d")
     gather_done("d")
-
-    partial_product(1, [(hidden_low, "d")])
     grad_hidden()
-    weight_grad("d", hidden_low)
-    sum_one("d")
-    partials[1].wait()
-    write_out()
-    partial_product(2, [(gate_part, "g"), (up_part, "u")])
-    transpose_rows(lambda columns: ff_in[:, columns])
-    weight_grad("g", gate_part)
+    feed_product(1, [(gate_part, "g"), (up_part, "u")])
+    transpose_rows(lambda columns: ff_in[:, :, columns], 2 * length)
+    weight_grad("g", lambda columns: gate_part[:, columns], 2 * length)
     sum_one("g")
-    weight_grad("u", up_part)
+    weight_grad("u", lambda columns: up_part[:, columns], 2 * length)
     sum_one("u")
-    partials[2].wait()
+    feed_wait(1)
     back_residual()
     proj_swap.start()
+    ff_spread.sent()
+    cot_spread.sent()
     sum_two("d")
     proj_swap.wait()
     back_mixed()
-    transpose_rows(lambda columns: grad_proj[:, columns])
-    weight_grad("o", at.mixed)
+    transpose_rows(lambda columns: grad_proj[:, columns], length)
+    weight_grad("o", lambda columns: at.mixed[:, columns], length)
     sum_one("o")
-    back_attend()
-    sum_three("d")
+    back_attend(0, 2)
     sum_two("g")
-    partial_product(3, [(grad_heads.at[:, pl.ds(0, WIDTHS["q"])], "q"),
-                        (grad_heads.at[:, pl.ds(WIDTHS["q"], WIDTHS["k"])], "k"),
-                        (grad_values, "v")])
-    transpose_rows(lambda columns: scaled[:, columns])
-    weight_grad("q", grad_heads)
+    back_attend(2, 4)
+    sum_two("u")
+    sum_four("d")
+    partial_product(
+        1,
+        [
+            (lambda rows: head_rows(0, rows, 0, WIDTHS["q"]), "q"),
+            (lambda rows: head_rows(8, rows, 0, WIDTHS["k"]), "k"),
+            (lambda rows: head_rows(8, rows, WIDTHS["k"], WIDTHS["v"]), "v"),
+        ],
+    )
+    transpose_rows(lambda columns: scaled[:, columns], length)
+    weight_grad("q", lambda columns: head_columns(0, columns), length)
     sum_one("q")
-    weight_grad("k", grad_heads, WIDTHS["q"])
+    weight_grad("k", lambda columns: head_columns(8, columns), length)
     sum_one("k")
-    weight_grad("v", grad_values)
+    weight_grad("v", lambda columns: head_columns(8, pl.ds(columns.start + WIDTHS["k"], 256)), length)
     sum_one("v")
-    partials[3].wait()
+    sum_two("o")
+    partials[1].wait()
     back_input()
     gain_grads()
     sum_one("e")
-    sum_three("g")
-    sum_two("u")
-    sum_four("d")
-    sum_three("u")
-    sum_two("o")
     sum_four("g")
+    feed_product(0, [(hidden_low, "d")])
+    feed_wait(0)
+    write_out()
     sum_three("o")
     sum_two("q")
     sum_four("u")
@@ -838,6 +966,7 @@
         sum_done(name)
     for copy in sum_sends:
         copy.wait_send()
+    gather_sent("d")
     hidden_move.sent()
     cot_move.sent()
     out_move.finish()
@@ -845,7 +974,7 @@
     assert places.count <= SEMAPHORES, places.count
 
 
-SEMAPHORES = 256
+SEMAPHORES = 320
 
 
 def fused(
@@ -905,11 +1034,11 @@
     block = (MB, tokens, D)
     outputs = dict(block_out=(block, BF, anywhere), input_grad=(block, BF, anywhere))
     for name, width in WIDTHS.items():
-        outputs["out_" + name] = ((rows, width if name == "e" else 2 * width), F32, vmem)
+        outputs["out_" + name] = ((rows, width * (4 if name in FEED else 1 if name == "e" else 2)), F32, vmem)
     own = 4 * tokens
     scratch = dict(
         hidden_own=((4, tokens, D), BF),
-        cot_all=((8, tokens, D), BF),
+        cot_all=((16, tokens, D), BF),
         seg_all=((8, 8, 2 * tokens), F32),
         gains=((8, D), F32),
         head_gains=((8, HD), F32),
@@ -925,26 +1054,35 @@
         mixed=((length, HALF_HQ * HD), BF),
         acc_own=((own, D), F32),
         partial_out=((2, own, D), BF),
-        partial_in=((4, own, D), BF),
+        partial_in=((2, own, D), BF),
+        near_out=((2, 2, own, D), BF),
+        near_in=((2, 2, own, D), BF),
+        cross_out=((2, own, D), BF),
+        cross_in=((2, own, D), BF),
         residual=((own, D), F32),
         grad_residual=((own, D), F32),
-        ff_in=((length, D), BF),
-        gate_part=((length, FF // 2), BF),
-        up_part=((length, FF // 2), BF),
-        hidden_low=((length, FF // 2), BF),
+        ff_in=((4, own, D), BF),
+        gate_part=((2 * length, FF // 4), BF),
+        up_part=((2 * length, FF // 4), BF),
+        hidden_low=((2 * length, FF // 4), BF),
+        grad_d=((2, 2, 4, 2, rows, FF // 4), BF),
         grad_proj=((length, D), BF),
-        grad_values=((length, HALF_HK * HD), BF),
         grad_key=((length, HD), F32),
         grad_value=((length, HD), F32),
         grad_query=((length, HD), F32),
-        turned_rows=((D, length), BF),
+        turned_rows=((D, 2 * length), BF),
         out_own=((4, tokens, D), BF),
         grad_own=((4, tokens, D), BF),
         r5_e=((rows, 128), F32),
     )
     for name, width in WIDTHS.items():
-        first, second = split_columns(name)
         scratch["w_" + name] = ((2, 2, 4, 2, rows, width), BF)
+        if name in FEED:
+            scratch["r1a_" + name] = ((2, 2, 4, rows, width), BF)
+            scratch["r3_" + name] = ((3, 2, 2, rows, width), BF)
+            scratch["r4_" + name] = ((3, rows, width), F32)
+            continue
+        first, second = split_columns(name, SUM_Y)
         scratch["r1a_" + name] = ((2, 2, 4, rows, first), BF)
         scratch["r2a_" + name] = ((2, 4, rows, first), BF)
         if second:

time: 397 us -> 332 us (0.84)
  Pallas kernels: 379 us -> 315 us
    pallas_call x1, Pallas kernels: 379 us -> 315 us  [fused(): pl.pallas_call(functools.partial(layer_kernel, names, tokens), out_shape=...]
where the time goes in v2:
time: 332 us; the launch traced here: 331 us
  Pallas kernels  315 us (95%)
  local copies, waits for them, and re-layouts  11.9 us (4%)
  other arithmetic  4.28 us (1%)
    pallas_call x1, Pallas kernels, fused(): pl.pallas_call(functools.partial(layer_kernel, names, tokens), out_shape=...  315 us
    unnamed x36, local copies, waits for them, and re-layouts  9.17 us

profile of v2, /device:TPU:0, one launch (start us, length us, event | category | flops | bytes accessed | tf_op | source)
XLA Modules:
  0.0 331.4 jit_solution(10290258581936796290)
XLA Ops:
  0.7 0.0 copy-start.10
  0.7 0.0 copy-start.11
  0.7 0.6 copy-done.10
  1.3 0.0 copy-done.11
  1.3 0.0 copy-start.12
  1.3 0.0 copy-start.13
  1.3 0.0 copy-start.9
  1.4 0.6 copy-done.12
  2.0 0.0 copy-done.13
  2.0 0.0 copy-done.9
  2.0 0.1 pad_select_fusion
  2.1 0.1 copy.39
  2.2 0.6 pad.15.refs_5_
  2.8 0.6 broadcast_in_dim.18.refs_2_
  3.4 1.0 fusion
  4.4 1.0 pad_maximum_fusion
  5.4 314.5 %layer.1 = (bf16[4,64,1024]{2,1,0:T(8,128)(2,1)}, bf16[4,64,1024]{2,1,0:T(8,128)(2,1)}, f32[32,128]{1,0:T(8,128)}, f32[32,1024]{1,0:T(8,128)}, f32[32,1024]{1,0:...) custom-call(bf16[4,64,1024]{2,1,0:T(8,128)(2,1)} %bitcast.22, ...), custom_call_target="tpu_custom_call" | custom-call | tf_op jit(solution)/shard_map/layer/pallas_call | solution.py:1094
  319.9 0.0 copy-start.8
  320.0 0.7 copy-done.8
  320.7 0.7 slice_reduce_fusion.2
  321.4 0.7 slice_reduce_fusion
  322.1 0.0 copy-start
  322.1 2.2 bitcast_convert_fusion
  324.3 0.0 copy-done
  324.3 0.0 copy-start.5
  324.3 0.8 copy.50
  325.1 0.3 copy-done.5
  325.4 0.0 copy-start.7
  325.4 0.0 copy-start.6
  325.4 0.7 copy.51
  326.1 0.3 copy-done.7
  326.4 0.0 copy-start.4
  326.4 0.7 copy.52
  327.0 0.0 copy-done.6
  327.0 0.0 copy-start.3
  327.0 0.7 copy.53
  327.7 0.0 copy-done.4
  327.7 0.7 copy.54
  328.4 0.0 copy-done.3
  328.4 0.0 copy-start.2
  328.4 0.7 copy.55
  329.1 0.4 copy-done.2
  329.5 0.0 copy-start.1
  329.5 0.7 copy.56
  330.3 0.4 copy-done.1
  330.7 0.7 copy.57
  (5 shorter events, 0.0 us)
Async XLA Ops:
  0.7 0.7 copy-start.10
  0.7 0.7 copy-start.11
  1.3 0.7 copy-start.12
  1.3 0.7 copy-start.13
  1.3 0.7 copy-start.9
  319.9 0.7 copy-start.8
  322.1 2.2 copy-start
  324.3 1.1 copy-start.5
  325.4 1.0 copy-start.7
  325.4 1.7 copy-start.6
  326.4 1.3 copy-start.4
  327.0 1.4 copy-start.3
  328.4 1.1 copy-start.2
  329.5 1.1 copy-start.1

commit v3 on v2

--- a/solution.py
+++ b/solution.py
@@ -3,6 +3,7 @@
 
 import jax
 import jax.numpy as jnp
+import numpy as np
 from jax import lax
 from jax.experimental import pallas as pl
 from jax.experimental.pallas import tpu as pltpu
@@ -41,10 +42,10 @@
     return positions[:, None] * frequency[None, :]
 
 
+KEYS = HK * HD // 2
 WIDTHS = dict(
-    e=128,
-    k=HK * HD // 2,
-    v=HK * HD // 2,
+    k=KEYS + 128,
+    v=KEYS,
     q=HQ * HD // 2,
     o=HQ * HD // 2,
     g=FF // 4,
@@ -53,13 +54,13 @@
 )
 ORDER = tuple(WIDTHS)
 FEED = ("g", "u", "d")
-GATHER_Y = dict(e=0, k=0, v=0, q=0, o=0)
-SUM_Y = dict(e=128, k=256, v=256, q=512, o=512)
+PIECES = dict(k=(256, 384), v=(512,), q=(512, 512), o=(512, 512), g=(768,), u=(768,), d=(384, 384))
+SUM_Y = dict(k=256, v=256, q=512, o=256)
 HALF_HQ, HALF_HK = HQ // 2, HK // 2
 
 
-def split_columns(name, by):
-    return by[name], WIDTHS[name] - by[name]
+def split_columns(name):
+    return SUM_Y[name], WIDTHS[name] - SUM_Y[name]
 
 
 def dot(left, right):
@@ -132,99 +133,136 @@
 
     weight = {n: getattr(at, "w_" + n) for n in ORDER}
     shard = {n: getattr(at, "in_" + n) for n in ORDER}
-    s0 = {n: places.take(3) for n in ORDER}
+    s0 = {n: places.take(3 if n in FEED else 1) for n in ORDER}
     lc = {n: places.take() for n in ORDER}
-    sz = {n: places.take(9) for n in ORDER}
-    s2 = {n: places.take(2) for n in ORDER}
-    s3 = {n: places.take(2) for n in ORDER}
+    pieces = []
+    for n in ORDER:
+        start = 0
+        for size in PIECES[n]:
+            pieces.append((n, pl.ds(start, size), places.take(4), places.take(), None if n in FEED else places.take()))
+            start += size
     gather_sends = {n: [] for n in ORDER}
 
     def part(name, xx, cc):
-        if name == "e":
-            return shard[name]
-        width = WIDTHS[name]
+        width = KEYS if name == "k" else WIDTHS[name]
         which = 2 * xx + cc if name in FEED else cc
         return shard[name].at[:, pl.ds(pl.multiple_of(which * width, width), width)]
 
+    def keys_at(ref):
+        return ref.at[:, pl.ds(0, KEYS)]
+
     def local(name):
+        if name == "k":
+            return pltpu.make_async_copy(part(name, x, c), keys_at(weight[name].at[x, c, z, y]), recvs.at[lc[name]])
         return pltpu.make_async_copy(part(name, x, c), weight[name].at[x, c, z, y], recvs.at[lc[name]])
 
     def begin(name, copy):
         copy.start()
         gather_sends[name].append(copy)
 
+    extra_place = places.take()
+
+    def gather_extra():
+        rows = at.share_rows
+        rows[...] = jnp.zeros_like(rows)
+        for i, gain in enumerate((at.attention_gain, at.feedforward_gain, at.query_gain, at.key_gain)):
+            rows[i : i + 1, : gain.shape[1]] = gain[...].astype(F32)
+        columns = rows[...].T[: at.extra.shape[0]].astype(BF)
+        at.extra[...] = columns
+        weight["k"][x, c, z, y, :, KEYS:] = columns
+        here = weight["k"].at[x, c, z, y, :, pl.ds(KEYS, 128)]
+        begin("k", remote(at.extra, here, extra_place, sibling))
+
     def gather_core(name):
         here = weight[name].at[x, c, z, y]
-        begin(name, remote(part(name, x, oc), here, s0[name], sibling))
+        begin(name, remote(part(name, x, oc), keys_at(here) if name == "k" else here, s0[name], sibling))
         if name in FEED:
             begin(name, remote(part(name, ox, c), here, s0[name] + 1, x_next))
             begin(name, remote(part(name, ox, oc), here, s0[name] + 2, x_cross))
         local(name).start()
 
-    def gather_z(name):
+    def gather_core_done(name):
         w = weight[name]
-        here = w.at[x, c, z, y]
-        for step in (1, 2, 3):
-            begin(name, remote(part(name, x, c), here, sz[name] + step - 1, z_device(step)))
-        block = w.at[x, oc, z, y]
-        arrived(block, s0[name], sibling)
-        for step in (1, 2, 3):
-            begin(name, remote(block, block, sz[name] + 2 + step, z_device(step)))
+        local(name).wait()
+        if name == "k":
+            arrived(keys_at(w.at[x, oc, z, y]), s0[name], sibling)
+        else:
+            arrived(w.at[x, oc, z, y], s0[name], sibling)
         if name in FEED:
             arrived(w.at[ox, c, z, y], s0[name] + 1, x_next)
             arrived(w.at[ox, oc, z, y], s0[name] + 2, x_cross)
-            block = w.at[ox, :, z, y]
-            for step in (1, 2, 3):
-                begin(name, remote(block, block, sz[name] + 5 + step, z_device(step)))
-
-    def gather_two(name):
+
+    middle = (z == 1) | (z == 2)
+    far = jnp.where(z == 1, 3, 0)
+
+    def z_block(piece, zz):
+        name, columns = piece[:2]
         w = weight[name]
-        local(name).wait()
-        for step in (1, 2, 3):
-            source = lax.rem(z + 4 - step, 4)
-            device = (dp, 2 * source + y)
-            arrived(w.at[x, c, source, y], sz[name] + step - 1, device)
-            arrived(w.at[x, oc, source, y], sz[name] + 2 + step, device)
-            if name in FEED:
-                arrived(w.at[ox, :, source, y], sz[name] + 5 + step, device)
-        if name in FEED:
-            block = w.at[:, :, :, y]
-            begin(name, remote(block, block, s2[name], y_next))
-            return
-        first, second = split_columns(name, GATHER_Y)
-        if first:
-            one = w.at[x, :, :, y, :, pl.ds(0, first)]
-            begin(name, remote(one, one, s2[name], x_next))
-        if second:
-            two = w.at[x, :, :, y, :, pl.ds(first, second)]
-            begin(name, remote(two, two, s2[name] + 1, y_next))
-
-    def gather_three(name):
+        return w.at[:, :, zz, y, :, columns] if name in FEED else w.at[x, :, zz, y, :, columns]
+
+    def z_copies(piece):
+        block = z_block(piece, z)
+        for there in range(4):
+            distance = jnp.abs(there - z)
+            sending = (distance == 1) | (distance == 2)
+            yield sending, lambda there=there: remote(
+                block, block, piece[2] + there, (dp, 2 * there + y), piece[2] + z
+            )
+
+    def z_forward(piece):
+        block = z_block(piece, far)
+        return remote(block, block, piece[2] + z, (dp, 2 * (3 - far) + y), piece[2] + far)
+
+    def gather_z(number):
+        piece = pieces[number]
+        if piece[1].start == 0:
+            gather_core_done(piece[0])
+        if number == 1:
+            arrived(weight["k"].at[x, oc, z, y, :, pl.ds(KEYS, 128)], extra_place, sibling)
+        for sending, copy in z_copies(piece):
+            pl.when(sending)(lambda copy=copy: copy().start())
+
+    def gather_two(number):
+        piece = pieces[number]
+        name, columns, sem, y_sem, _ = piece
         w = weight[name]
-        first, second = split_columns(name, GATHER_Y)
-        if first:
-            arrived(w.at[ox, :, :, y, :, pl.ds(0, first)], s2[name], x_next)
-            one = w.at[:, :, :, y, :, pl.ds(0, first)]
-            begin(name, remote(one, one, s3[name], y_next))
-        if second:
-            arrived(w.at[x, :, :, oy, :, pl.ds(first, second)], s2[name] + 1, y_next)
-            two = w.at[x, :, :, :, :, pl.ds(first, second)]
-            begin(name, remote(two, two, s3[name] + 1, x_next))
+
+        @pl.when(middle)
+        def _():
+            arrived(z_block(piece, far), sem + far, (dp, 2 * far + y))
+            z_forward(piece).start()
+
+        for source in range(4):
+            waiting = (z != source) & jnp.logical_not(middle & (far == source))
+            pl.when(waiting)(
+                lambda source=source: arrived(z_block(piece, source), sem + source, (dp, 2 * source + y))
+            )
+        block = w.at[:, :, :, y, :, columns] if name in FEED else w.at[x, :, :, y, :, columns]
+        begin(name, remote(block, block, y_sem, y_next))
+
+    def gather_three(number):
+        name, columns, _, y_sem, x_sem = pieces[number]
+        w = weight[name]
+        arrived(w.at[x, :, :, oy, :, columns], y_sem, y_next)
+        block = w.at[x, :, :, :, :, columns]
+        begin(name, remote(block, block, x_sem, x_next))
 
     def gather_done(name):
         w = weight[name]
-        if name in FEED:
-            arrived(w.at[:, :, :, oy], s2[name], y_next)
-            return
-        first, second = split_columns(name, GATHER_Y)
-        if first:
-            arrived(w.at[:, :, :, oy, :, pl.ds(0, first)], s3[name], y_next)
-        if second:
-            arrived(w.at[ox, :, :, :, :, pl.ds(first, second)], s3[name] + 1, x_next)
+        for piece in pieces:
+            if piece[0] == name and name in FEED:
+                arrived(w.at[:, :, :, oy, :, piece[1]], piece[3], y_next)
+            elif piece[0] == name:
+                arrived(w.at[ox, :, :, :, :, piece[1]], piece[4], x_next)
 
     def gather_sent(name):
         for copy in gather_sends[name]:
             copy.wait_send()
+        for piece in pieces:
+            if piece[0] == name:
+                for sending, copy in z_copies(piece):
+                    pl.when(sending)(lambda copy=copy: copy().wait_send())
+                pl.when(middle)(lambda piece=piece: z_forward(piece).wait_send())
 
     slot = 2 * lax.rem(z, 2) + y
     target_core = lax.div(z, 2)
@@ -306,47 +344,12 @@
                     lambda m=m, device=device: arrived(self.landing.at[m], self.recv + m, device)
                 )
 
-    hidden_own, cot_all, seg_all = at.hidden_own, at.cot_all, at.seg_all
+    hidden_own, cot_all = at.hidden_own, at.cot_all
     hidden_move = Reshard(at.hidden_in, lambda core, j: hidden_own.at[j])
+    number_move = Reshard(at.number_out, lambda core, j: at.number_own.at[j])
     cot_move = Reshard(at.cotangent, lambda core, j: cot_all.at[4 * (2 * x + core) + j])
     out_move = Return(at.out_own, at.block_out)
     grad_move = Return(at.grad_own, at.input_grad)
-    seg_place, seg_recv, seg_own = places.take(8), places.take(8), places.take()
-
-    def seg_cases():
-        for m in range(MB):
-            for core in range(2):
-                keeps = (core == c) & (z == m) & (y == c)
-                yield m, core, keeps
-
-    def seg_copy(m, core):
-        return remote(
-            at.segments.at[m], seg_all.at[ctx], seg_place + 2 * m + core, (2 * x + core, 2 * m + c), seg_recv + ctx
-        )
-
-    def seg_start():
-        for m, core, keeps in seg_cases():
-            pl.when(jnp.logical_not(keeps))(lambda m=m, core=core: seg_copy(m, core).start())
-            pl.when(keeps)(
-                lambda m=m: pltpu.make_async_copy(
-                    at.segments.at[m], seg_all.at[ctx], recvs.at[seg_own]
-                ).start()
-            )
-
-    def seg_wait():
-        for m, core, keeps in seg_cases():
-            pl.when(jnp.logical_not(keeps))(lambda m=m, core=core: seg_copy(m, core).wait_send())
-        for j in range(8):
-            mine = (y == c) & (ctx == j)
-            pl.when(jnp.logical_not(mine))(
-                lambda j=j: arrived(seg_all.at[j], seg_recv + j, (2 * x + y, j))
-            )
-            pl.when(mine)(
-                lambda j=j: pltpu.make_async_copy(
-                    seg_all.at[j], seg_all.at[j], recvs.at[seg_own]
-                ).wait()
-            )
-
     class Swap:
         def __init__(self, source, there, here):
             self.place = places.take()
@@ -395,10 +398,10 @@
             for copy in (self.near, self.across, self.far):
                 copy.wait_send()
 
-    r1 = {n: places.take(2) for n in ORDER}
-    r2 = {n: places.take(2) for n in ORDER}
-    r3 = {n: places.take(3) for n in ORDER}
-    r4 = {n: places.take(3) for n in ORDER}
+    r1 = {n: places.take(1 if n in FEED else 2) for n in ORDER}
+    r2 = {n: places.take(0 if n in FEED else 2) for n in ORDER}
+    r3 = {n: places.take(4) for n in ORDER}
+    r4 = {n: places.take(3 if n in FEED else 1) for n in ORDER}
     sum_sends = []
     grads = dict(weight, d=at.grad_d)
 
@@ -406,19 +409,55 @@
         copy.start()
         sum_sends.append(copy)
 
+    def sum_block(name, zz):
+        w = grads[name]
+        return w.at[:, :, zz, y] if name in FEED else w.at[x, :, zz, y]
+
+    end = jnp.logical_not(middle)
+    neighbour = jnp.where(z == 0, 1, 2)
+
+    def sum_z_copies(name):
+        landing = getattr(at, "r3_" + name)
+        for there in range(4):
+            distance = jnp.abs(there - z)
+            sending = (distance == 1) | ((distance == 2) & end)
+            yield sending, lambda there=there: remote(
+                sum_block(name, there), landing.at[z], r3[name] + there, (dp, 2 * there + y), r3[name] + z
+            )
+
+        yield end, lambda: remote(
+            sum_block(name, 3 - z), landing.at[neighbour], r3[name] + z, (dp, 2 * neighbour + y), r3[name] + neighbour
+        )
+
+    def sum_z_late(name):
+        landing = getattr(at, "r3_" + name)
+        return remote(sum_block(name, far), landing.at[z], r3[name] + far, (dp, 2 * far + y), r3[name] + z)
+
     def sum_z(name):
-        w = grads[name]
-        for step in (1, 2, 3):
-            there = z_at(step)
-            block = w.at[:, :, there, y] if name in FEED else w.at[x, :, there, y]
-            send(remote(block, getattr(at, "r3_" + name).at[step - 1], r3[name] + step - 1, z_device(step)))
+        for sending, copy in sum_z_copies(name):
+            pl.when(sending)(lambda copy=copy: copy().start())
+
+    def sum_z_pass(name):
+        landing, w = getattr(at, "r3_" + name), grads[name]
+
+        @pl.when(middle)
+        def _():
+            arrived(landing.at[z], r3[name] + z, (dp, 2 * (3 - far) + y))
+            if name in FEED:
+                for xx in range(2):
+                    for cc in range(2):
+                        w[xx, cc, far, y] += landing[z, xx, cc]
+            else:
+                for cc in range(2):
+                    w[x, cc, far, y] += landing[z, cc]
+            sum_z_late(name).start()
 
     def sum_one(name):
         w = grads[name]
         if name in FEED:
             send(remote(w.at[:, :, :, oy], getattr(at, "r1a_" + name), r1[name], y_next))
             return
-        first, second = split_columns(name, SUM_Y)
+        first, second = split_columns(name)
         send(remote(w.at[:, :, :, oy, :, pl.ds(0, first)], getattr(at, "r1a_" + name), r1[name], y_next))
         if second:
             send(remote(w.at[ox, :, :, :, :, pl.ds(first, second)], getattr(at, "r1b_" + name), r1[name] + 1, x_next))
@@ -426,7 +465,7 @@
     def sum_two(name):
         w = grads[name]
         arrived(getattr(at, "r1a_" + name), r1[name], y_next)
-        first, second = (WIDTHS[name], 0) if name in FEED else split_columns(name, SUM_Y)
+        first, second = (WIDTHS[name], 0) if name in FEED else split_columns(name)
 
         @pl.loop(0, 16)
         def _(i):
@@ -449,7 +488,7 @@
 
     def sum_three(name):
         w = grads[name]
-        first, second = split_columns(name, SUM_Y)
+        first, second = split_columns(name)
         arrived(getattr(at, "r2a_" + name), r2[name], x_next)
         if second:
             arrived(getattr(at, "r2b_" + name), r2[name] + 1, y_next)
@@ -465,15 +504,19 @@
 
     def sum_four(name):
         w, landed = grads[name], getattr(at, "r3_" + name)
-        for step in (1, 2, 3):
-            arrived(landed.at[step - 1], r3[name] + step - 1, (dp, 2 * lax.rem(z + 4 - step, 4) + y))
+        for source in range(4):
+            coming = (z != source) & (jnp.abs(source - z) != 3)
+            pl.when(coming)(
+                lambda source=source: arrived(landed.at[source], r3[name] + source, (dp, 2 * source + y))
+            )
 
         def total(*place):
             mine = w[(*place, z, y)] if name in FEED else w[(x, *place, z, y)]
             value = mine.astype(F32)
-            for step in range(3):
-                value = value + landed[(step, *place)].astype(F32)
-            return value
+            value = value + landed[(jnp.where(z == 0, 1, z - 1), *place)].astype(F32)
+            value = value + landed[(jnp.where(z == 0, 2, jnp.where(z == 3, 1, z + 1)), *place)].astype(F32)
+            third = landed[(far, *place)].astype(F32)
+            return jnp.where(middle, value + third, value)
 
         width = WIDTHS[name]
         staged, result = getattr(at, "r4_" + name), getattr(at, "out_" + name)
@@ -485,20 +528,13 @@
             result[:, columns] = total(x, c)
             return
         staged[...] = total(oc)
-        if name == "e":
-            send(remote(staged, at.r5_e, r4[name], sibling))
-            result[...] = total(c)
-        else:
-            columns = pl.ds(pl.multiple_of(c * width, width), width)
-            send(remote(staged, result.at[:, columns], r4[name], sibling))
-            result[:, columns] = total(c)
+        columns = pl.ds(pl.multiple_of(c * width, width), width)
+        send(remote(staged, result.at[:, columns], r4[name], sibling))
+        result[:, columns] = total(c)
 
     def sum_done(name):
         width = WIDTHS[name]
-        if name == "e":
-            arrived(at.r5_e, r4[name], sibling)
-            at.out_e[...] = at.out_e[...] + at.r5_e[...]
-        elif name in FEED:
+        if name in FEED:
             for i, (xx, cc, device) in enumerate(((ox, oc, x_cross), (ox, c, x_next), (x, oc, sibling))):
                 columns = pl.ds(pl.multiple_of((2 * xx + cc) * width, width), width)
                 arrived(getattr(at, "out_" + name).at[:, columns], r4[name] + i, device)
@@ -530,21 +566,28 @@
         return jnp.where(hit, 1.0, 0.0).astype(BF)
 
     def prepare_gains():
-        columns = weight["e"][...].reshape(D, 128).astype(F32)
+        columns = weight["k"][:, :, :, :, :, KEYS:].reshape(D, 128).astype(F32)
         for i in range(8):
             gains[:, i * 128 : (i + 1) * 128] = columns[i * 128 : (i + 1) * 128].T[:8]
         head_gains[...] = dot(gains[...].astype(BF), selector())
 
+    def prepare_numbers():
+        for m in range(MB):
+            at.share_rows[:1, :tokens] = at.segments[m].astype(F32)
+            at.number_out[m] = jnp.broadcast_to(at.share_rows[:1], (128, 128)).T[:tokens].astype(BF)
+
     def prepare_mask():
-        rows = [seg_all[2 * j, 0:1] + seg_all[2 * j + 1, 0:1] for j in range(4)]
-        for i in range(4):
-            query = jnp.broadcast_to(rows[i], (128, 128)).T
-            for j in range(4):
+        def number(i):
+            return scaled[i * 128 : (i + 1) * 128, D:].astype(F32)
+
+        for j in range(4):
+            key = number(j).T
+            for i in range(4):
                 place = slice(i * 128, (i + 1) * 128), slice(j * 128, (j + 1) * 128)
                 if j > i:
                     at.bias[place] = jnp.full((128, 128), MASKED, F32)
                     continue
-                seen = query == jnp.broadcast_to(rows[j], (128, 128))
+                seen = number(i) == key
                 if i == j:
                     seen = seen & (
                         lax.broadcasted_iota(jnp.int32, (128, 128), 1)
@@ -562,12 +605,15 @@
         @pl.loop(0, 4)
         def _(j):
             value = normalize(hidden_own[j].astype(F32)) * gains[0:1]
-            scaled[own_block(j)] = value.astype(BF)
+            scaled[own_block(j), :D] = value.astype(BF)
+            scaled[own_block(j), D:] = at.number_own[j]
 
     def columns_of(name, t, size=256):
         return weight[name][:, :, :, :, :, pl.ds(pl.multiple_of(t * size, size), size)].reshape(D, size)
 
     def rows_of(name, t):
+        if name == "k":
+            return weight[name][lax.div(t, 2), lax.rem(t, 2), :, :, :, :KEYS].reshape(D // 4, KEYS)
         return weight[name][lax.div(t, 2), lax.rem(t, 2)].reshape(D // 4, WIDTHS[name])
 
     cosine, sine = at.cosine, at.sine
@@ -575,10 +621,10 @@
     def turn(value):
         return value * cosine[...] + pltpu.roll(value, HD // 2, 1) * sine[...]
 
-    def project_heads(name, gain, kept, turned):
-        @pl.loop(0, WIDTHS[name] // 256)
+    def project_heads(name, count, gain, kept, turned):
+        @pl.loop(0, count // 2)
         def _(t):
-            both = dot(scaled[...], columns_of(name, t))
+            both = dot(scaled[:, :D], columns_of(name, t))
             for i in range(2):
                 value = both[:, i * HD : (i + 1) * HD]
                 kept[2 * t + i] = value
@@ -587,7 +633,7 @@
     def project_values():
         @pl.loop(0, WIDTHS["v"] // 256)
         def _(t):
-            both = dot(scaled[...], columns_of("v", t))
+            both = dot(scaled[:, :D], columns_of("v", t))
             for i in range(2):
                 at.values[2 * t + i] = both[:, i * HD : (i + 1) * HD].astype(BF)
 
@@ -729,7 +775,7 @@
         if name != "d":
             gather_sent(name)
 
-        @pl.loop(0, WIDTHS[name] // 256)
+        @pl.loop(0, (KEYS if name == "k" else WIDTHS[name]) // 256)
         def _(t):
             columns = pl.ds(pl.multiple_of(t * 256, 256), 256)
             grad = dot(turned_rows[:, :count], right(columns))
@@ -811,7 +857,7 @@
                 back_head(at.query_acc[head], grad_query[...], 2, 0, lanes)
             lanes = pl.ds(pl.multiple_of(pair * HD, HD), HD)
             back_head(at.key_acc[pair], grad_key[...], 3, 8, lanes)
-            put_heads(8, pl.ds(pl.multiple_of(WIDTHS["k"] + pair * HD, HD), HD), grad_value[...])
+            put_heads(8, pl.ds(pl.multiple_of(KEYS + pair * HD, HD), HD), grad_value[...])
 
     def back_input():
         @pl.loop(0, 4)
@@ -828,74 +874,84 @@
             grad_move.start(j)
 
     def gain_grads():
-        gather_sent("e")
         grad_gains[...] += dot_nt(grad_head_gains[...].astype(BF), selector())
         for i in range(8):
             block = jnp.concatenate(
                 [grad_gains[:, i * 128 : (i + 1) * 128], jnp.zeros((120, 128), F32)], axis=0
             ).T
-            weight["e"][i // 4, (i // 2) % 2, 2 * (i % 2) : 2 * (i % 2) + 2] = block.astype(BF).reshape(2, 2, 32, 128)
-
-    for name in ("e", "k", "v", "q", "o"):
+            weight["k"][i // 4, (i // 2) % 2, 2 * (i % 2) : 2 * (i % 2) + 2, :, :, KEYS:] = block.astype(BF).reshape(
+                2, 2, 32, 128
+            )
+
+    gather_core("k")
+    gather_extra()
+    gather_z(0)
+    gather_core("v")
+    gather_z(1)
+    for name in ("q", "o", *FEED):
         gather_core(name)
-    gather_z("e")
-    gather_z("k")
-    seg_start()
+    prepare_numbers()
+    gather_two(0)
+    gather_z(2)
+    gather_two(1)
+    gather_three(0)
+    gather_z(3)
+    gather_two(2)
+    gather_three(1)
+    gather_z(4)
     hidden_move.start()
-    gather_two("e")
-    gather_z("v")
-    gather_two("k")
-    gather_z("q")
-    gather_three("e")
-    gather_two("v")
-    gather_three("k")
-    gather_z("o")
-    gather_done("e")
+    number_move.start()
+    gather_two(3)
+    gather_three(2)
+    gather_z(5)
+    gather_two(4)
+    gather_three(3)
+    gather_z(6)
+    gather_two(5)
+    gather_three(4)
+    gather_z(7)
+    gather_done("k")
     prepare_gains()
-    seg_wait()
-    prepare_mask()
     hidden_move.wait()
+    number_move.wait()
     scale_input()
     scaled_swap.start()
-    gather_two("q")
-    for name in FEED:
-        gather_core(name)
-    gather_z("g")
-    gather_three("v")
-    gather_done("k")
+    gather_two(6)
+    gather_three(5)
+    gather_z(8)
     scaled_swap.wait()
-    project_heads("k", head_gains[3:4], at.key_acc, at.keys)
-    gather_two("o")
-    gather_three("q")
-    cot_move.start()
+    prepare_mask()
+    project_heads("k", HALF_HK, head_gains[3:4], at.key_acc, at.keys)
     gather_done("v")
     project_values()
-    gather_two("g")
-    gather_z("u")
-    gather_three("o")
+    gather_three(6)
+    gather_two(7)
+    gather_z(9)
     gather_done("q")
-    project_heads("q", head_gains[2:3], at.query_acc, at.queries)
-    cot_move.wait()
-    cot_spread.start()
+    project_heads("q", HALF_HQ, head_gains[2:3], at.query_acc, at.queries)
+    gather_two(8)
+    gather_z(10)
+    cot_move.start()
     attend(0, 4)
-    gather_two("u")
-    gather_z("d")
-    cot_spread.pass_on()
+    gather_two(9)
     attend(4, 8)
     gather_done("o")
     partial_product(0, [(lambda rows: at.mixed[rows], "o")])
+    gather_two(10)
     partials[0].wait()
     add_residual()
     ff_spread.start()
-    gather_two("d")
-    cot_spread.near_wait()
-    cot_spread.far_wait()
-    transpose_rows(lambda columns: cot_all[:, :, columns], 2 * length)
+    cot_move.wait()
+    cot_spread.start()
     gather_done("g")
     gather_done("u")
     ff_spread.near_wait()
     feed_forward(x)
     ff_spread.pass_on()
+    cot_spread.pass_on()
+    cot_spread.near_wait()
+    cot_spread.far_wait()
+    transpose_rows(lambda columns: cot_all[:, :, columns], 2 * length)
     ff_spread.far_wait()
     feed_forward(ox)
 
@@ -922,59 +978,69 @@
     sum_one("o")
     back_attend(0, 2)
     sum_two("g")
+    sum_z_pass("d")
     back_attend(2, 4)
     sum_two("u")
-    sum_four("d")
+    sum_z_pass("g")
     partial_product(
         1,
         [
             (lambda rows: head_rows(0, rows, 0, WIDTHS["q"]), "q"),
-            (lambda rows: head_rows(8, rows, 0, WIDTHS["k"]), "k"),
-            (lambda rows: head_rows(8, rows, WIDTHS["k"], WIDTHS["v"]), "v"),
+            (lambda rows: head_rows(8, rows, 0, KEYS), "k"),
+            (lambda rows: head_rows(8, rows, KEYS, KEYS), "v"),
         ],
     )
     transpose_rows(lambda columns: scaled[:, columns], length)
     weight_grad("q", lambda columns: head_columns(0, columns), length)
     sum_one("q")
+    weight_grad("v", lambda columns: head_columns(8, pl.ds(columns.start + KEYS, 256)), length)
+    sum_one("v")
     weight_grad("k", lambda columns: head_columns(8, columns), length)
-    sum_one("k")
-    weight_grad("v", lambda columns: head_columns(8, pl.ds(columns.start + WIDTHS["k"], 256)), length)
-    sum_one("v")
-    sum_two("o")
     partials[1].wait()
     back_input()
     gain_grads()
-    sum_one("e")
-    sum_four("g")
+    sum_one("k")
+    sum_two("o")
+    sum_z_pass("u")
+    sum_four("d")
     feed_product(0, [(hidden_low, "d")])
     feed_wait(0)
     write_out()
     sum_three("o")
+    sum_four("g")
     sum_two("q")
+    sum_z_pass("o")
     sum_four("u")
     sum_three("q")
+    sum_two("v")
+    sum_z_pass("q")
+    sum_four("o")
+    sum_three("v")
     sum_two("k")
-    sum_four("o")
+    sum_z_pass("v")
+    sum_four("q")
     sum_three("k")
-    sum_two("v")
-    sum_two("e")
-    sum_three("v")
-    sum_three("e")
-    for name in ("q", "k", "v", "e"):
-        sum_four(name)
-    for name in ("d", "g", "u", "o", "q", "k", "v", "e"):
+    sum_z_pass("k")
+    sum_four("v")
+    sum_four("k")
+    for name in ("d", "g", "u", "o", "q", "v", "k"):
         sum_done(name)
     for copy in sum_sends:
         copy.wait_send()
+    for name in ORDER:
+        for sending, copy in sum_z_copies(name):
+            pl.when(sending)(lambda copy=copy: copy().wait_send())
+        pl.when(middle)(lambda name=name: sum_z_late(name).wait_send())
     gather_sent("d")
     hidden_move.sent()
+    number_move.sent()
     cot_move.sent()
     out_move.finish()
     grad_move.finish()
-    assert places.count <= SEMAPHORES, places.count
-
-
-SEMAPHORES = 320
+    assert places.count == SEMAPHORES, places.count
+
+
+SEMAPHORES = 204
 
 
 def fused(
@@ -996,33 +1062,24 @@
     tokens = hidden_in.shape[2]
     length = 8 * tokens
     rows = query_weight.shape[0]
-    odd = lax.rem(lax.axis_index("ctx"), 2)
-    numbers = segments[:, 0].astype(F32)
-    blank = jnp.zeros_like(numbers)
-    numbers = jnp.where(
-        odd == 0, jnp.concatenate([numbers, blank], axis=1), jnp.concatenate([blank, numbers], axis=1)
-    )
-    numbers = jnp.broadcast_to(numbers[:, None], (MB, 8, 2 * tokens))
-
-    def column(gain):
-        return jnp.pad(gain, (0, rows - gain.shape[0]))
-
-    extra = jnp.stack(
-        [attention_gain, feedforward_gain, column(query_gain), column(key_gain)], axis=1
-    )
-    extra = jnp.pad(extra, ((0, 0), (0, 124)))
-    angles = rope_angles(0, length)
-    cosine = jnp.concatenate([jnp.cos(angles), jnp.cos(angles)], axis=-1)
-    sine = jnp.concatenate([-jnp.sin(angles), jnp.sin(angles)], axis=-1)
+    heads = query_gain.shape[0]
+    positions = np.arange(length, dtype=np.float32)
+    frequency = (ROPE_BASE ** (-(np.arange(HD // 2, dtype=np.float32) * 2.0) / HD)).astype(np.float32)
+    angles = (positions[:, None] * frequency[None, :]).astype(np.float64)
+    cosine = np.concatenate([np.cos(angles), np.cos(angles)], axis=-1).astype(np.float32)
+    sine = np.concatenate([-np.sin(angles), np.sin(angles)], axis=-1).astype(np.float32)
 
     vmem, anywhere = pl.BlockSpec(memory_space=pltpu.VMEM), pl.BlockSpec(memory_space=pl.ANY)
     inputs = dict(
         hidden_in=(hidden_in[:, 0], anywhere),
         cotangent=(cotangent[:, 0], anywhere),
-        segments=(numbers, vmem),
-        cosine=(cosine, vmem),
-        sine=(sine, vmem),
-        in_e=(extra, anywhere),
+        segments=(segments, vmem),
+        cosine=(jnp.asarray(cosine), vmem),
+        sine=(jnp.asarray(sine), vmem),
+        attention_gain=(attention_gain[None], vmem),
+        feedforward_gain=(feedforward_gain[None], vmem),
+        query_gain=(query_gain[None], vmem),
+        key_gain=(key_gain[None], vmem),
         in_k=(key_weight, anywhere),
         in_v=(value_weight, anywhere),
         in_q=(query_weight, anywhere),
@@ -1034,18 +1091,21 @@
     block = (MB, tokens, D)
     outputs = dict(block_out=(block, BF, anywhere), input_grad=(block, BF, anywhere))
     for name, width in WIDTHS.items():
-        outputs["out_" + name] = ((rows, width * (4 if name in FEED else 1 if name == "e" else 2)), F32, vmem)
+        outputs["out_" + name] = ((rows, width * (4 if name in FEED else 2)), F32, vmem)
     own = 4 * tokens
     scratch = dict(
+        share_rows=((128, 128), F32),
+        extra=((rows, 128), BF),
+        number_out=((MB, tokens, 128), BF),
+        number_own=((4, tokens, 128), BF),
         hidden_own=((4, tokens, D), BF),
         cot_all=((16, tokens, D), BF),
-        seg_all=((8, 8, 2 * tokens), F32),
         gains=((8, D), F32),
         head_gains=((8, HD), F32),
         grad_gains=((8, D), F32),
         grad_head_gains=((8, HD), F32),
         bias=((length, length), F32),
-        scaled=((length, D), BF),
+        scaled=((length, D + 128), BF),
         query_acc=((HALF_HQ, length, HD), F32),
         key_acc=((HALF_HK, length, HD), F32),
         queries=((HALF_HQ, length, HD), BF),
@@ -1073,22 +1133,21 @@
         turned_rows=((D, 2 * length), BF),
         out_own=((4, tokens, D), BF),
         grad_own=((4, tokens, D), BF),
-        r5_e=((rows, 128), F32),
     )
     for name, width in WIDTHS.items():
         scratch["w_" + name] = ((2, 2, 4, 2, rows, width), BF)
         if name in FEED:
             scratch["r1a_" + name] = ((2, 2, 4, rows, width), BF)
-            scratch["r3_" + name] = ((3, 2, 2, rows, width), BF)
+            scratch["r3_" + name] = ((4, 2, 2, rows, width), BF)
             scratch["r4_" + name] = ((3, rows, width), F32)
             continue
-        first, second = split_columns(name, SUM_Y)
+        first, second = split_columns(name)
         scratch["r1a_" + name] = ((2, 2, 4, rows, first), BF)
         scratch["r2a_" + name] = ((2, 4, rows, first), BF)
         if second:
             scratch["r1b_" + name] = ((2, 4, 2, rows, second), BF)
             scratch["r2b_" + name] = ((2, 4, rows, second), BF)
-        scratch["r3_" + name] = ((3, 2, rows, width), BF)
+        scratch["r3_" + name] = ((4, 2, rows, width), BF)
         scratch["r4_" + name] = ((rows, width), F32)
     names = (*inputs, *outputs, *scratch, "sends", "recvs")
     results = pl.pallas_call(
@@ -1103,24 +1162,92 @@
         ),
         name="layer",
     )(*(value for value, _ in inputs.values()))
-    got = types.SimpleNamespace(**dict(zip(outputs, results)))
-    gain_grads = got.out_e
-    heads = query_gain.shape[0]
+    got = finish(types.SimpleNamespace(**dict(zip(outputs, results))), rows, heads)
     return (
         got.block_out[:, None],
-        got.input_grad.astype(F32)[:, None],
-        gain_grads[:, 0],
-        gain_grads[:heads, 2],
-        gain_grads[:heads, 3],
+        got.input_grad[:, None],
+        got.attention_gain[0],
+        got.query_gain[0],
+        got.key_gain[0],
         got.out_q,
         got.out_k,
         got.out_v,
         got.out_o.T,
-        gain_grads[:, 1],
+        got.feedforward_gain[0],
         got.out_g,
         got.out_u,
         got.out_d.T,
     )
+
+
+def finish_kernel(names, heads, *refs):
+    at = types.SimpleNamespace(**dict(zip(names, refs)))
+    moved = [n[4:] for n in names if n.startswith("got_")]
+    brought = [
+        pltpu.make_async_copy(getattr(at, "got_" + n), getattr(at, "here_" + n), at.brought.at[i])
+        for i, n in enumerate(moved)
+    ]
+    for copy in brought:
+        copy.start()
+    taken = []
+
+    def take(name, source):
+        copy = pltpu.make_async_copy(source, getattr(at, name), at.taken.at[len(taken)])
+        copy.start()
+        taken.append(copy)
+
+    def ready(name):
+        brought[moved.index(name)].wait()
+        return getattr(at, "here_" + name)
+
+    value = ready("input_grad")
+    for m in range(MB):
+        at.wide_grad[m] = value[m].astype(F32)
+    take("input_grad", at.wide_grad)
+    for name in moved:
+        if name not in ("input_grad", "out_k"):
+            take(name, ready(name))
+    value = ready("out_k")
+    at.keys[:, :KEYS] = value[:, :KEYS]
+    at.keys[:, KEYS:] = value[:, KEYS + 128 : 2 * KEYS + 128]
+    take("out_k", at.keys)
+    gains = value[:, KEYS : KEYS + 128] + value[:, 2 * KEYS + 128 :]
+    blank = jnp.zeros((128 - gains.shape[0], 128), F32)
+    turned = jnp.concatenate([gains, blank], axis=0).T
+    at.attention_gain[...] = turned[0:1, : gains.shape[0]]
+    at.feedforward_gain[...] = turned[1:2, : gains.shape[0]]
+    at.query_gain[...] = turned[2:3, :heads]
+    at.key_gain[...] = turned[3:4, :heads]
+    for copy in taken:
+        copy.wait()
+
+
+def finish(got, rows, heads):
+    vmem, anywhere = pl.BlockSpec(memory_space=pltpu.VMEM), pl.BlockSpec(memory_space=pl.ANY)
+    inputs = vars(got)
+    outputs = {n: (v.shape, v.dtype, anywhere) for n, v in inputs.items()}
+    outputs.update(
+        input_grad=(got.input_grad.shape, F32, anywhere),
+        out_k=((rows, 2 * KEYS), F32, anywhere),
+        attention_gain=((1, rows), F32, vmem),
+        feedforward_gain=((1, rows), F32, vmem),
+        query_gain=((1, heads), F32, vmem),
+        key_gain=((1, heads), F32, vmem),
+    )
+    scratch = {"here_" + n: (v.shape, v.dtype) for n, v in inputs.items()}
+    scratch.update(wide_grad=(got.input_grad.shape, F32), keys=((rows, 2 * KEYS), F32))
+    names = (*("got_" + n for n in inputs), *outputs, *scratch, "brought", "taken")
+    results = pl.pallas_call(
+        functools.partial(finish_kernel, names, heads),
+        out_shape=[jax.ShapeDtypeStruct(shape, dtype) for shape, dtype, _ in outputs.values()],
+        in_specs=[anywhere] * len(inputs),
+        out_specs=[spec for _, _, spec in outputs.values()],
+        scratch_shapes=[pltpu.VMEM(shape, dtype) for shape, dtype in scratch.values()]
+        + [pltpu.SemaphoreType.DMA((len(inputs),))] * 2,
+        compiler_params=pltpu.CompilerParams(vmem_limit_bytes=64 * 2**20 - 2**16),
+        name="results",
+    )(*inputs.values())
+    return types.SimpleNamespace(**dict(zip(outputs, results)))
 
 
 def rope_tables(first, count):

time: 332 us -> 291 us (0.88)
  Pallas kernels: 315 us -> 289 us
  local copies, waits for them, and re-layouts: 11.9 us -> 0 us
  other arithmetic: 4.28 us -> 0 us
    pallas_call x1, Pallas kernels: 315 us -> 285 us  [fused(): pl.pallas_call(functools.partial(layer_kernel, names, tokens), out_shape=...]
    unnamed x36 -> x0, local copies, waits for them, and re-layouts: 9.17 us -> none
    pallas_call x0 -> x1, Pallas kernels: none -> 3.73 us  [finish(): pl.pallas_call(functools.partial(finish_kernel, names, heads), out_shape=...]
where the time goes in v3:
time: 291 us; the launch traced here: 290 us
  Pallas kernels  289 us (99%)
    pallas_call x1, Pallas kernels, fused(): pl.pallas_call(functools.partial(layer_kernel, names, tokens), out_shape=...  285 us

profile of v3, /device:TPU:0, one launch (start us, length us, event | category | flops | bytes accessed | tf_op | source)
XLA Modules:
  0.0 290.0 jit_solution(17468442890914330839)
XLA Ops:
  0.7 285.4 %layer.1 = (bf16[4,64,1024]{2,1,0:T(8,128)(2,1)}, bf16[4,64,1024]{2,1,0:T(8,128)(2,1)}, f32[32,1280]{1,0:T(8,128)}, f32[32,1024]{1,0:T(8,128)}, f32[32,2048]{1,0...) custom-call(bf16[4,64,1024]{2,1,0:T(8,128)(2,1)} %bitcast.20, ...), custom_call_target="tpu_custom_call" | custom-call | tf_op jit(solution)/shard_map/layer/pallas_call | solution.py:1153
  286.1 3.7 %results.1 = (bf16[4,64,1024]{2,1,0:T(8,128)(2,1)}, f32[4,64,1024]{2,1,0:T(8,128)}, f32[32,1024]{1,0:T(8,128)}, f32[32,1024]{1,0:T(8,128)}, f32[32,2048]{1,0:T(8...) custom-call(bf16[4,64,1024]{2,1,0:T(8,128)(2,1)} %get-tuple-element., ...), custom_call_target="tpu_custom_call" | custom-call | tf_op jit(solution)/shard_map/results/pallas_call | solution.py:1240

commit v4 on v3

--- a/solution.py
+++ b/solution.py
@@ -55,7 +55,8 @@
 ORDER = tuple(WIDTHS)
 FEED = ("g", "u", "d")
 PIECES = dict(k=(256, 384), v=(512,), q=(512, 512), o=(512, 512), g=(768,), u=(768,), d=(384, 384))
-SUM_Y = dict(k=256, v=256, q=512, o=256)
+X_FIRST = (2,)
+SUM_Y = dict(k=256, v=256, q=512, o=128)
 HALF_HQ, HALF_HK = HQ // 2, HK // 2
 
 
@@ -238,22 +239,29 @@
                 lambda source=source: arrived(z_block(piece, source), sem + source, (dp, 2 * source + y))
             )
         block = w.at[:, :, :, y, :, columns] if name in FEED else w.at[x, :, :, y, :, columns]
-        begin(name, remote(block, block, y_sem, y_next))
+        begin(name, remote(block, block, y_sem, x_next if number in X_FIRST else y_next))
 
     def gather_three(number):
         name, columns, _, y_sem, x_sem = pieces[number]
         w = weight[name]
+        if number in X_FIRST:
+            arrived(w.at[ox, :, :, y, :, columns], y_sem, x_next)
+            block = w.at[:, :, :, y, :, columns]
+            begin(name, remote(block, block, x_sem, y_next))
+            return
         arrived(w.at[x, :, :, oy, :, columns], y_sem, y_next)
         block = w.at[x, :, :, :, :, columns]
         begin(name, remote(block, block, x_sem, x_next))
 
-    def gather_done(name):
+    def gather_done(number):
+        name, columns, _, y_sem, x_sem = pieces[number]
         w = weight[name]
-        for piece in pieces:
-            if piece[0] == name and name in FEED:
-                arrived(w.at[:, :, :, oy, :, piece[1]], piece[3], y_next)
-            elif piece[0] == name:
-                arrived(w.at[ox, :, :, :, :, piece[1]], piece[4], x_next)
+        if name in FEED:
+            arrived(w.at[:, :, :, oy, :, columns], y_sem, y_next)
+        elif number in X_FIRST:
+            arrived(w.at[:, :, :, oy, :, columns], x_sem, y_next)
+        else:
+            arrived(w.at[ox, :, :, :, :, columns], x_sem, x_next)
 
     def gather_sent(name):
         for copy in gather_sends[name]:
@@ -523,8 +531,8 @@
         if name in FEED:
             columns = pl.ds(pl.multiple_of(dp * width, width), width)
             for i, (xx, cc, device) in enumerate(((ox, oc, x_cross), (ox, c, x_next), (x, oc, sibling))):
-                staged[i] = total(xx, cc)
-                send(remote(staged.at[i], result.at[:, columns], r4[name] + i, device))
+                staged[i] = total(xx, cc).astype(BF)
+                send(remote(staged.at[i], getattr(at, "r5_" + name).at[i], r4[name] + i, device))
             result[:, columns] = total(x, c)
             return
         staged[...] = total(oc)
@@ -537,7 +545,8 @@
         if name in FEED:
             for i, (xx, cc, device) in enumerate(((ox, oc, x_cross), (ox, c, x_next), (x, oc, sibling))):
                 columns = pl.ds(pl.multiple_of((2 * xx + cc) * width, width), width)
-                arrived(getattr(at, "out_" + name).at[:, columns], r4[name] + i, device)
+                arrived(getattr(at, "r5_" + name).at[i], r4[name] + i, device)
+                getattr(at, "out_" + name)[:, columns] = getattr(at, "r5_" + name)[i].astype(F32)
         else:
             columns = pl.ds(pl.multiple_of(oc * width, width), width)
             arrived(getattr(at, "out_" + name).at[:, columns], r4[name], sibling)
@@ -678,6 +687,8 @@
         return acc_own[here_block(j)] + at.partial_in[index, here_block(j)].astype(F32)
 
     def feed_product(index, terms):
+        acc = at.acc_feed if index == 0 else acc_own
+
         def rows_times(xx, cc, t):
             first = pl.multiple_of((2 * xx + cc) * own_rows, own_rows)
             return sum(dot_nt(left[pl.ds(first, own_rows)], rows_of(name, t)) for left, name in terms)
@@ -691,7 +702,7 @@
 
         def keep(xx):
             def body(t, columns):
-                acc_own[:, columns] = rows_times(xx, c, t)
+                acc[:, columns] = rows_times(xx, c, t)
 
             column_quarters(body)
 
@@ -703,9 +714,10 @@
         @pl.loop(0, 4)
         def _(j):
             rows = here_block(j)
-            at.cross_out[index, rows] = (acc_own[rows] + near[index, 0, rows].astype(F32)).astype(BF)
-
-        feed_cross[index][0].start()
+            at.cross_out[index, rows] = (acc[rows] + near[index, 0, rows].astype(F32)).astype(BF)
+
+        if index == 1:
+            feed_cross[index][0].start()
         give(1, x)
         keep(x)
 
@@ -717,7 +729,8 @@
 
     def feed_sum(index, j):
         rows = here_block(j)
-        return acc_own[rows] + at.near_in[index, 1, rows].astype(F32) + at.cross_in[index, rows].astype(F32)
+        acc = at.acc_feed if index == 0 else acc_own
+        return acc[rows] + at.near_in[index, 1, rows].astype(F32) + at.cross_in[index, rows].astype(F32)
 
     def add_residual():
         @pl.loop(0, 4)
@@ -905,29 +918,31 @@
     gather_three(2)
     gather_z(5)
     gather_two(4)
+    gather_z(6)
+    gather_done(0)
+    gather_done(1)
     gather_three(3)
-    gather_z(6)
+    prepare_gains()
     gather_two(5)
-    gather_three(4)
     gather_z(7)
-    gather_done("k")
-    prepare_gains()
     hidden_move.wait()
     number_move.wait()
     scale_input()
     scaled_swap.start()
     gather_two(6)
-    gather_three(5)
     gather_z(8)
     scaled_swap.wait()
     prepare_mask()
     project_heads("k", HALF_HK, head_gains[3:4], at.key_acc, at.keys)
-    gather_done("v")
+    gather_done(2)
+    gather_three(4)
     project_values()
-    gather_three(6)
     gather_two(7)
     gather_z(9)
-    gather_done("q")
+    gather_done(3)
+    gather_three(5)
+    gather_done(4)
+    gather_three(6)
     project_heads("q", HALF_HQ, head_gains[2:3], at.query_acc, at.queries)
     gather_two(8)
     gather_z(10)
@@ -935,36 +950,37 @@
     attend(0, 4)
     gather_two(9)
     attend(4, 8)
-    gather_done("o")
+    gather_done(5)
+    gather_done(6)
     partial_product(0, [(lambda rows: at.mixed[rows], "o")])
-    gather_two(10)
     partials[0].wait()
     add_residual()
     ff_spread.start()
+    gather_two(10)
     cot_move.wait()
     cot_spread.start()
-    gather_done("g")
-    gather_done("u")
+    gather_done(7)
+    gather_done(8)
     ff_spread.near_wait()
     feed_forward(x)
     ff_spread.pass_on()
+    ff_spread.far_wait()
+    feed_forward(ox)
     cot_spread.pass_on()
     cot_spread.near_wait()
     cot_spread.far_wait()
     transpose_rows(lambda columns: cot_all[:, :, columns], 2 * length)
-    ff_spread.far_wait()
-    feed_forward(ox)
 
     weight_grad("d", lambda columns: hidden_low[:, columns], 2 * length)
     sum_one("d")
-    gather_done("d")
+    gather_done(9)
+    gather_done(10)
     grad_hidden()
     feed_product(1, [(gate_part, "g"), (up_part, "u")])
     transpose_rows(lambda columns: ff_in[:, :, columns], 2 * length)
     weight_grad("g", lambda columns: gate_part[:, columns], 2 * length)
     sum_one("g")
     weight_grad("u", lambda columns: up_part[:, columns], 2 * length)
-    sum_one("u")
     feed_wait(1)
     back_residual()
     proj_swap.start()
@@ -976,12 +992,11 @@
     transpose_rows(lambda columns: grad_proj[:, columns], length)
     weight_grad("o", lambda columns: at.mixed[:, columns], length)
     sum_one("o")
+    sum_one("u")
     back_attend(0, 2)
     sum_two("g")
     sum_z_pass("d")
     back_attend(2, 4)
-    sum_two("u")
-    sum_z_pass("g")
     partial_product(
         1,
         [
@@ -993,24 +1008,27 @@
     transpose_rows(lambda columns: scaled[:, columns], length)
     weight_grad("q", lambda columns: head_columns(0, columns), length)
     sum_one("q")
+    sum_two("o")
     weight_grad("v", lambda columns: head_columns(8, pl.ds(columns.start + KEYS, 256)), length)
+    weight_grad("k", lambda columns: head_columns(8, columns), length)
+    sum_two("u")
     sum_one("v")
-    weight_grad("k", lambda columns: head_columns(8, columns), length)
+    feed_product(0, [(hidden_low, "d")])
+    feed_cross[0][0].start()
     partials[1].wait()
     back_input()
     gain_grads()
+    sum_z_pass("g")
+    sum_four("d")
+    sum_three("o")
+    sum_z_pass("u")
+    sum_four("g")
+    sum_two("q")
     sum_one("k")
-    sum_two("o")
-    sum_z_pass("u")
-    sum_four("d")
-    feed_product(0, [(hidden_low, "d")])
+    sum_z_pass("o")
+    sum_four("u")
     feed_wait(0)
     write_out()
-    sum_three("o")
-    sum_four("g")
-    sum_two("q")
-    sum_z_pass("o")
-    sum_four("u")
     sum_three("q")
     sum_two("v")
     sum_z_pass("q")
@@ -1020,8 +1038,8 @@
     sum_z_pass("v")
     sum_four("q")
     sum_three("k")
+    sum_four("v")
     sum_z_pass("k")
-    sum_four("v")
     sum_four("k")
     for name in ("d", "g", "u", "o", "q", "v", "k"):
         sum_done(name)
@@ -1113,6 +1131,7 @@
         values=((HALF_HK, length, HD), BF),
         mixed=((length, HALF_HQ * HD), BF),
         acc_own=((own, D), F32),
+        acc_feed=((own, D), F32),
         partial_out=((2, own, D), BF),
         partial_in=((2, own, D), BF),
         near_out=((2, 2, own, D), BF),
@@ -1139,7 +1158,8 @@
         if name in FEED:
             scratch["r1a_" + name] = ((2, 2, 4, rows, width), BF)
             scratch["r3_" + name] = ((4, 2, 2, rows, width), BF)
-            scratch["r4_" + name] = ((3, rows, width), F32)
+            scratch["r4_" + name] = ((3, rows, width), BF)
+            scratch["r5_" + name] = ((3, rows, width), BF)
             continue
         first, second = split_columns(name)
         scratch["r1a_" + name] = ((2, 2, 4, rows, first), BF)

time: 291 us -> 265 us (0.911)
  Pallas kernels: 289 us -> 264 us
    pallas_call x1, Pallas kernels: 285 us -> 260 us  [fused(): pl.pallas_call(functools.partial(layer_kernel, names, tokens), out_shape=...]
where the time goes in v4:
time: 265 us
  Pallas kernels  264 us (100%)
    pallas_call x1, Pallas kernels, fused(): pl.pallas_call(functools.partial(layer_kernel, names, tokens), out_shape=...  260 us

profile of v4, /device:TPU:0, one launch (start us, length us, event | category | flops | bytes accessed | tf_op | source)
XLA Modules:
  0.0 264.9 jit_solution(2178793148338240132)
XLA Ops:
  0.7 260.4 %layer.1 = (bf16[4,64,1024]{2,1,0:T(8,128)(2,1)}, bf16[4,64,1024]{2,1,0:T(8,128)(2,1)}, f32[32,1280]{1,0:T(8,128)}, f32[32,1024]{1,0:T(8,128)}, f32[32,2048]{1,0...) custom-call(bf16[4,64,1024]{2,1,0:T(8,128)(2,1)} %bitcast.20, ...), custom_call_target="tpu_custom_call" | custom-call | tf_op jit(solution)/shard_map/layer/pallas_call | solution.py:1173
  261.1 3.7 %results.1 = (bf16[4,64,1024]{2,1,0:T(8,128)(2,1)}, f32[4,64,1024]{2,1,0:T(8,128)}, f32[32,1024]{1,0:T(8,128)}, f32[32,1024]{1,0:T(8,128)}, f32[32,2048]{1,0:T(8...) custom-call(bf16[4,64,1024]{2,1,0:T(8,128)(2,1)} %get-tuple-element., ...), custom_call_target="tpu_custom_call" | custom-call | tf_op jit(solution)/shard_map/results/pallas_call | solution.py:1260

commit v5 on v4

--- a/solution.py
+++ b/solution.py
@@ -55,7 +55,7 @@
 ORDER = tuple(WIDTHS)
 FEED = ("g", "u", "d")
 PIECES = dict(k=(256, 384), v=(512,), q=(512, 512), o=(512, 512), g=(768,), u=(768,), d=(384, 384))
-X_FIRST = (2,)
+X_FIRST = (3,)
 SUM_Y = dict(k=256, v=256, q=512, o=128)
 HALF_HQ, HALF_HK = HQ // 2, HK // 2
 

time: 265 us -> 265 us (level)
  no operation moved by 1% of the time
where the time goes in v5:
time: 265 us; the launch traced here: 264 us
  Pallas kernels  263 us (99%)
    pallas_call x1, Pallas kernels, fused(): pl.pallas_call(functools.partial(layer_kernel, names, tokens), out_shape=...  260 us

profile of v5, /device:TPU:0, one launch (start us, length us, event | category | flops | bytes accessed | tf_op | source)
XLA Modules:
  0.0 264.2 jit_solution(11141198296466496660)
XLA Ops:
  0.7 259.6 %layer.1 = (bf16[4,64,1024]{2,1,0:T(8,128)(2,1)}, bf16[4,64,1024]{2,1,0:T(8,128)(2,1)}, f32[32,1280]{1,0:T(8,128)}, f32[32,1024]{1,0:T(8,128)}, f32[32,2048]{1,0...) custom-call(bf16[4,64,1024]{2,1,0:T(8,128)(2,1)} %bitcast.20, ...), custom_call_target="tpu_custom_call" | custom-call | tf_op jit(solution)/shard_map/layer/pallas_call | solution.py:1173
  260.3 3.7 %results.1 = (bf16[4,64,1024]{2,1,0:T(8,128)(2,1)}, f32[4,64,1024]{2,1,0:T(8,128)}, f32[32,1024]{1,0:T(8,128)}, f32[32,1024]{1,0:T(8,128)}, f32[32,2048]{1,0:T(8...) custom-call(bf16[4,64,1024]{2,1,0:T(8,128)(2,1)} %get-tuple-element., ...), custom_call_target="tpu_custom_call" | custom-call | tf_op jit(solution)/shard_map/results/pallas_call | solution.py:1260
